TPU v7x, 32 devices: a whole 2x2x4 slice. The times are simulated.
32 devices in a mesh: orbit: 2 (over x), lon: 4 (over y, core), lat: 4 (over z).
Axes of the slice: x: 2, y: 2, z: 4, core: 2. Of those that a mesh axis runs over, the one named last changes fastest.
Arguments:
- observed: float32 [4096, 64], P(('orbit', 'lon', 'lat')), may hold values from -6 to 6
- ray_start: int32 [4096], P(('orbit', 'lon', 'lat')), may hold values from 0 to 2
- tile_cells: int32 [20480, 16], P(('orbit', 'lon', 'lat')), may hold values from 0 to 4095, as said below
- tile_lengths: float32 [20480, 16], P(('orbit', 'lon', 'lat')), may hold values from 0.05 to 0.2
- channel_kernel: float32 [7, 64], replicated, may hold values from -0.75 to 0.75
- noise_weight: float32 [64], replicated, may hold values from 0.25 to 4
- prior_weight: float32 [7], replicated, may hold values from 0.05 to 0.5
Outputs:
- solution_field: float32 [7, 16, 32, 128], P(None, 'lon', 'lat')
- residual: float32 [7, 16, 32, 128], P(None, 'lon', 'lat')
Inputs may be any that keep to these rules, and one draw needn't show every extreme that they name: `tile_cells`: each row is a path through the block: its segments move across the block's longitudes at one latitude, their level falling to a tangent level and rising again, one level a segment.
All inputs are finite; a program needn't handle non-finite values.
Results may differ from a plain program's by a relative error of at most 0.0045.
Values sent between devices are 32-bit elements; how exact they have to be, the bound alone decides.
A program may use at most 64 MiB of HBM per device.

v0:
```python
import jax
import jax.numpy as jnp
from jax import lax
from jax.sharding import PartitionSpec as P

CLON = 4
CLAT = 8
LEV = 128
NT = 3
ITERS = 4


highest = lax.Precision.HIGHEST


def padded_2(array, sides, width):
    for axis, dim in sides:
        size, length = (lax.axis_size(axis), array.shape[dim])
        up = [(i, (i + 1) % size) for i in range(size)]
        down = [(j, i) for i, j in up]
        last = lax.slice_in_dim(array, length - width, length, axis=dim)
        first = lax.slice_in_dim(array, 0, width, axis=dim)
        before = lax.ppermute(last, axis, up)
        after = lax.ppermute(first, axis, down)
        array = jnp.concatenate([before, array, after], axis=dim)
    return array


def passed_along(block, axis, distance):
    devices = range(lax.axis_size(axis))
    route = [((i - distance) % len(devices), i) for i in devices]
    return lax.ppermute(block, axis, route)


def prior_term(field_part, lower_level, upper_level, prior_weight):
    padded = padded_2(field_part, (("lon", 1), ("lat", 2)), 1)
    lat_count = field_part.shape[2]
    lat_rows = lax.broadcasted_iota(jnp.int32, (1, 1, lat_count, 1), 2)
    lat_index = lax.axis_index("lat")
    south_side = jnp.where((lat_rows == 0) & (lat_index == 0), 0.0, padded[:, 1:-1, :-2, :])
    north_side = jnp.where(
        (lat_rows == lat_count - 1) & (lat_index == lax.axis_size("lat") - 1),
        0.0,
        padded[:, 1:-1, 2:, :],
    )
    neighbours = padded[:, :-2, 1:-1, :] + padded[:, 2:, 1:-1, :]
    neighbours = neighbours + south_side + north_side + lower_level + upper_level
    return prior_weight[:, None, None, None] * (6.0 * field_part - neighbours)


def body(observed, ray_start, tile_cells, tile_lengths, channel_kernel, noise_weight, prior_weight):
    ray_count = ray_start.shape[0]
    species = channel_kernel.shape[0]
    reach = NT - 1
    span = 2 * NT - 1
    cell_count = CLON * CLAT * LEV
    field_shape = (species, CLON, CLAT, LEV)
    slot_rows = jnp.arange(span, dtype=jnp.int32)[:, None]
    crossing = (
        (ray_start[None, :] <= slot_rows) & (ray_start[None, :] + reach >= slot_rows)
    ).astype(jnp.float32)
    cells_across = jnp.transpose(tile_cells)
    lengths_across = jnp.transpose(tile_lengths)
    cell_places = cells_across.reshape(-1)
    weighted = channel_kernel * noise_weight[None, :]
    channel_gram = jnp.dot(weighted, channel_kernel.T, precision=highest)

    def spread(ray_image):
        arrived = []
        for slot in range(span):
            offset = slot - reach
            outgoing = ray_image * crossing[slot][None, :]
            if offset == 0:
                arrived.append(outgoing)
            else:
                arrived.append(passed_along(outgoing, "lon", offset))
        stacked = jnp.stack(arrived, axis=1).reshape(species, span * ray_count)
        amounts = (stacked[:, None, :] * lengths_across[None]).reshape(species, -1)
        deposited = jnp.zeros((species, cell_count), jnp.float32).at[:, cell_places].add(amounts)
        return deposited.reshape(field_shape)

    slab_size = LEV
    slab_start = 0

    def global_sums(terms):
        return lax.psum((terms[0],), ("lon", "lat"))

    ray_source = lax.dot_general(weighted, observed, (((1,), (1,)), ((), ())), precision=highest)
    rhs_full = lax.psum(spread(ray_source), "orbit")
    solution = jnp.zeros_like(rhs_full)
    residual = rhs_full
    direction = rhs_full
    (norm_now,) = global_sums((jnp.sum(residual * residual),))
    for turn_index in range(ITERS):
        operand = rhs_full if turn_index == 0 else direction
        flat_field = operand.reshape(species, cell_count)
        values = flat_field[:, cells_across]
        tile_totals = jnp.sum(values * lengths_across[None], axis=1).reshape(
            species, span, ray_count
        )
        projected = jnp.zeros((species, ray_count), jnp.float32)
        for normal_slot in range(span):
            normal_offset = normal_slot - reach
            piece = tile_totals[:, normal_slot]
            if normal_offset != 0:
                piece = passed_along(piece, "lon", -normal_offset)
            projected = projected + piece * crossing[normal_slot][None, :]
        partial_image = spread(jnp.dot(channel_gram, projected, precision=highest))
        summed = lax.psum(partial_image, "orbit")
        padded = jnp.pad(operand, ((0, 0), (0, 0), (0, 0), (1, 1)))
        lower_level = lax.dynamic_slice_in_dim(padded, slab_start, slab_size, 3)
        upper_level = lax.dynamic_slice_in_dim(padded, slab_start + 2, slab_size, 3)
        image_field = summed + prior_term(operand, lower_level, upper_level, prior_weight)
        (curvature,) = global_sums((jnp.sum(direction * image_field),))
        step_size = norm_now / curvature
        solution = solution + step_size * direction
        residual = residual - step_size * image_field
        (norm_next,) = global_sums((jnp.sum(residual * residual),))
        direction = residual + norm_next / norm_now * direction
        norm_now = norm_next
    return (solution, residual)


def solution(mesh):
    return jax.shard_map(
        body,
        mesh=mesh,
        in_specs=(
            P(("orbit", "lon", "lat"), None),
            P(("orbit", "lon", "lat")),
            P(("orbit", "lon", "lat"), None),
            P(("orbit", "lon", "lat"), None),
            P(),
            P(),
            P(),
        ),
        out_specs=(P(None, "lon", "lat", None), P(None, "lon", "lat", None)),
        check_vma=False,
    )
```

profile of v0, /device:TPU:0, one launch (start us, length us, event | category | flops | bytes accessed | tf_op | source)
XLA Modules:
  0.0 891.7 jit_solution(15148327341693382020)
XLA Ops:
  9.4 3.0 collective-permute-start
  16.7 10.6 %bitcast_multiply_fusion.4 = f32[7,10240]{0,1:T(8,128)} fusion(f32[10240]{0:T(1024)S(1)} %mul.263, f32[7,640]{0,1:T(8,128)S(1)} %copy.32), kind=kLoop, calls=%fused_computation.23 | loop fusion | flops 71680 | bytes 345600 | tf_op jit(solution)/shard_map/mul | solution.py:78
  27.2 50.7 %scatter_custom_fusion = f32[7,4096]{0,1:T(8,128)S(1)} fusion(s32[10240]{0:T(1024)S(1)} %bitcast.241, f32[7,10240]{0,1:T(8,128)} %bitcast_multiply_fusion.4, f32[]{:T(128)} %constant.8.clone.1), kind=kCustom, calls=%fused_computation.21 | custom fusion | flops 71680 | bytes 401412 | tf_op jit(solution)/shard_map/scatter-add | solution.py:79
  79.3 22.1 %all-reduce.11.cloned.1.call-done = f32[7,4,8,128]{3,2,1,0:T(8,128)} async-done(((f32[7,4,8,128]{3,2,1,0:T(8,128)}), f32[7,4,8,128]{3,2,1,0:T(8,128)}) %all-reduce.11.cloned.1.call-update) | async-done | bytes 114704 | tf_op jit(solution)/shard_map/psum | solution.py:89
  101.5 1.6 copy.34
  103.1 34.3 %gather_fusion = f32[10240,7]{1,0:T(8,128)} fusion(f32[7,4096]{0,1:T(8,128)S(1)} %bitcast.210, s32[10240]{0:T(1024)S(1)} %broadcast_clamp_fusion), kind=kCustom, calls=%fused_computation | custom fusion | bytes 614400 | tf_op jit(solution)/shard_map/gather | solution.py:97
  137.4 4.1 multiply_reduce_fusion.3
  141.6 1.5 collective-permute-start.7
  148.0 1.7 collective-permute-start.13
  152.8 1.8 collective-permute-done.11
  154.8 10.6 %bitcast_multiply_fusion.3 = f32[7,10240]{0,1:T(8,128)} fusion(f32[7,640]{0,1:T(8,128)S(1)} %copy.36, f32[10240]{0:T(1024)S(1)} %mul.263), kind=kLoop, calls=%fused_computation.20 | loop fusion | flops 71680 | bytes 345600 | tf_op jit(solution)/shard_map/mul | solution.py:78
  165.4 50.7 %scatter_custom_fusion.1 = f32[7,4096]{0,1:T(8,128)S(1)} fusion(s32[10240]{0:T(1024)S(1)} %bitcast.242, f32[7,10240]{0,1:T(8,128)} %bitcast_multiply_fusion.3, f32[]{:T(128)} %constant.8.clone.1), kind=kCustom, calls=%fused_computation.18 | custom fusion | flops 71680 | bytes 401412 | tf_op jit(solution)/shard_map/scatter-add | solution.py:79
  217.5 3.4 collective-permute-start.15
  220.9 1.5 collective-permute-done.15
  222.4 4.1 collective-permute-done.14
  226.5 11.5 %all-reduce.13.cloned.1.call-done = f32[7,4,8,128]{3,2,1,0:T(8,128)} async-done(((f32[7,4,8,128]{3,2,1,0:T(8,128)}), f32[7,4,8,128]{3,2,1,0:T(8,128)}) %all-reduce.13.cloned.1.call-update) | async-done | bytes 114704 | tf_op jit(solution)/shard_map/psum | solution.py:109
  238.0 1.7 multiply_reduce_fusion.10
  239.7 33.5 %all-reduce.4 = (f32[]{:T(128)}, f32[]{:T(128)}) all-reduce(f32[]{:T(128)} %get-tuple-element.3, f32[]{:T(128)} %get-tuple-element.2), channel_id=1, replica_groups=mesh['orbit'=2,'lon'=4,'lat'=4] {'lon','lat'}, use_global_device_ids=true, to_apply=%region_3.0 | all-reduce | flops 2 | bytes 16 | tf_op jit(solution)/shard_map/psum | solution.py:86
  275.2 30.3 %psum.95 = f32[]{:T(128)} all-reduce(f32[]{:T(128)} %multiply_reduce_fusion.9), channel_id=1, replica_groups=mesh['orbit'=2,'lon'=4,'lat'=4] {'lon','lat'}, use_global_device_ids=true, to_apply=%region_10.11 | all-reduce | flops 1 | bytes 8 | tf_op jit(solution)/shard_map/psum | solution.py:86
  307.5 34.3 %gather_fusion.1 = f32[10240,7]{1,0:T(8,128)} fusion(f32[7,4096]{0,1:T(8,128)S(1)} %bitcast.211, s32[10240]{0:T(1024)S(1)} %broadcast_clamp_fusion), kind=kCustom, calls=%fused_computation.1 | custom fusion | bytes 614400 | tf_op jit(solution)/shard_map/gather | solution.py:97
  341.8 4.1 multiply_reduce_fusion.2
  358.2 10.6 %bitcast_multiply_fusion.2 = f32[7,10240]{0,1:T(8,128)} fusion(f32[7,640]{0,1:T(8,128)S(1)} %copy.40, f32[10240]{0:T(1024)S(1)} %mul.263), kind=kLoop, calls=%fused_computation.17 | loop fusion | flops 71680 | bytes 345600 | tf_op jit(solution)/shard_map/mul | solution.py:78
  368.8 50.7 %scatter_custom_fusion.2 = f32[7,4096]{0,1:T(8,128)S(1)} fusion(s32[10240]{0:T(1024)S(1)} %bitcast.243, f32[7,10240]{0,1:T(8,128)} %bitcast_multiply_fusion.2, f32[]{:T(128)} %constant.8.clone.1), kind=kCustom, calls=%fused_computation.15 | custom fusion | flops 71680 | bytes 401412 | tf_op jit(solution)/shard_map/scatter-add | solution.py:79
  423.3 1.7 collective-permute-done.27
  425.0 2.9 collective-permute-done.26
  427.9 13.3 %all-reduce.15.cloned.1.call-done = f32[7,4,8,128]{3,2,1,0:T(8,128)} async-done(((f32[7,4,8,128]{3,2,1,0:T(8,128)}), f32[7,4,8,128]{3,2,1,0:T(8,128)}) %all-reduce.15.cloned.1.call-update) | async-done | bytes 114704 | tf_op jit(solution)/shard_map/psum | solution.py:109
  441.1 1.6 multiply_reduce_fusion.8
  442.8 33.5 %psum.97 = f32[]{:T(128)} all-reduce(f32[]{:T(128)} %get-tuple-element.14), channel_id=1, replica_groups=mesh['orbit'=2,'lon'=4,'lat'=4] {'lon','lat'}, use_global_device_ids=true, to_apply=%region_15.16 | all-reduce | flops 1 | bytes 8 | tf_op jit(solution)/shard_map/psum | solution.py:86
  478.3 30.3 %psum.98 = f32[]{:T(128)} all-reduce(f32[]{:T(128)} %get-tuple-element.12), channel_id=1, replica_groups=mesh['orbit'=2,'lon'=4,'lat'=4] {'lon','lat'}, use_global_device_ids=true, to_apply=%region_17.18 | all-reduce | flops 1 | bytes 8 | tf_op jit(solution)/shard_map/psum | solution.py:86
  510.6 34.3 %gather_fusion.2 = f32[10240,7]{1,0:T(8,128)} fusion(f32[7,4096]{0,1:T(8,128)S(1)} %bitcast.212, s32[10240]{0:T(1024)S(1)} %broadcast_clamp_fusion), kind=kCustom, calls=%fused_computation.2 | custom fusion | bytes 614400 | tf_op jit(solution)/shard_map/gather | solution.py:97
  544.8 4.1 multiply_reduce_fusion.1
  561.3 10.6 %bitcast_multiply_fusion.1 = f32[7,10240]{0,1:T(8,128)} fusion(f32[7,640]{0,1:T(8,128)S(1)} %copy.44, f32[10240]{0:T(1024)S(1)} %mul.263), kind=kLoop, calls=%fused_computation.14 | loop fusion | flops 71680 | bytes 345600 | tf_op jit(solution)/shard_map/mul | solution.py:78
  571.9 50.7 %scatter_custom_fusion.3 = f32[7,4096]{0,1:T(8,128)S(1)} fusion(s32[10240]{0:T(1024)S(1)} %bitcast.244, f32[7,10240]{0,1:T(8,128)} %bitcast_multiply_fusion.1, f32[]{:T(128)} %constant.8.clone.1), kind=kCustom, calls=%fused_computation.12 | custom fusion | flops 71680 | bytes 401412 | tf_op jit(solution)/shard_map/scatter-add | solution.py:79
  626.4 1.7 collective-permute-done.39
  628.1 2.9 collective-permute-done.38
  631.0 13.3 %all-reduce.17.cloned.1.call-done = f32[7,4,8,128]{3,2,1,0:T(8,128)} async-done(((f32[7,4,8,128]{3,2,1,0:T(8,128)}), f32[7,4,8,128]{3,2,1,0:T(8,128)}) %all-reduce.17.cloned.1.call-update) | async-done | bytes 114704 | tf_op jit(solution)/shard_map/psum | solution.py:109
  644.2 1.6 multiply_reduce_fusion.6
  645.9 33.5 %psum.100 = f32[]{:T(128)} all-reduce(f32[]{:T(128)} %get-tuple-element.10), channel_id=1, replica_groups=mesh['orbit'=2,'lon'=4,'lat'=4] {'lon','lat'}, use_global_device_ids=true, to_apply=%region_22.23 | all-reduce | flops 1 | bytes 8 | tf_op jit(solution)/shard_map/psum | solution.py:86
  681.3 30.3 %psum.101 = f32[]{:T(128)} all-reduce(f32[]{:T(128)} %get-tuple-element.8), channel_id=1, replica_groups=mesh['orbit'=2,'lon'=4,'lat'=4] {'lon','lat'}, use_global_device_ids=true, to_apply=%region_24.25 | all-reduce | flops 1 | bytes 8 | tf_op jit(solution)/shard_map/psum | solution.py:86
  713.7 34.3 %gather_fusion.3 = f32[10240,7]{1,0:T(8,128)} fusion(f32[7,4096]{0,1:T(8,128)S(1)} %bitcast.209, s32[10240]{0:T(1024)S(1)} %broadcast_clamp_fusion), kind=kCustom, calls=%fused_computation.3 | custom fusion | bytes 614400 | tf_op jit(solution)/shard_map/gather | solution.py:97
  748.0 4.1 multiply_reduce_fusion
  764.4 10.6 %bitcast_multiply_fusion = f32[7,10240]{0,1:T(8,128)} fusion(f32[7,640]{0,1:T(8,128)S(1)} %copy.48, f32[10240]{0:T(1024)S(1)} %mul.263), kind=kLoop, calls=%fused_computation.11 | loop fusion | flops 71680 | bytes 345600 | tf_op jit(solution)/shard_map/mul | solution.py:78
  775.0 50.7 %scatter_custom_fusion.4 = f32[7,4096]{0,1:T(8,128)S(1)} fusion(s32[10240]{0:T(1024)S(1)} %bitcast.245, f32[7,10240]{0,1:T(8,128)} %bitcast_multiply_fusion, f32[]{:T(128)} %constant.8.clone.1), kind=kCustom, calls=%fused_computation.9 | custom fusion | flops 71680 | bytes 401412 | tf_op jit(solution)/shard_map/scatter-add | solution.py:79
  829.5 1.7 collective-permute-done.51
  831.2 2.8 collective-permute-done.50
  834.0 13.3 %all-reduce.19.cloned.1.call-done = f32[7,4,8,128]{3,2,1,0:T(8,128)} async-done(((f32[7,4,8,128]{3,2,1,0:T(8,128)}), f32[7,4,8,128]{3,2,1,0:T(8,128)}) %all-reduce.19.cloned.1.call-update) | async-done | bytes 114704 | tf_op jit(solution)/shard_map/psum | solution.py:109
  847.3 1.6 multiply_reduce_fusion.4
  849.0 33.5 %psum.103 = f32[]{:T(128)} all-reduce(f32[]{:T(128)} %get-tuple-element.6), channel_id=1, replica_groups=mesh['orbit'=2,'lon'=4,'lat'=4] {'lon','lat'}, use_global_device_ids=true, to_apply=%region_29.30 | all-reduce | flops 1 | bytes 8 | tf_op jit(solution)/shard_map/psum | solution.py:86
  (196 shorter events, 71.1 us)
Async XLA Ops:
  7.2 94.3 %all-reduce.11.cloned.1.call-start = ((), (), s32[]{:S(2)}) async-start(), calls=%async_computation | async-start | bytes 229376 | tf_op jit(solution)/shard_map/psum | solution.py:89
  9.4 6.6 collective-permute-start
  12.4 3.7 collective-permute-start.1
  12.4 3.7 collective-permute-start.2
  12.9 3.6 collective-permute-start.3
  79.3 158.8 %all-reduce.13.cloned.1.call-start = ((), (), s32[]{:S(2)}) async-start(), calls=%async_computation.1 | async-start | bytes 229376 | tf_op jit(solution)/shard_map/psum | solution.py:109
  141.6 3.7 collective-permute-start.7
  143.6 3.6 collective-permute-start.4
  147.4 3.6 collective-permute-start.8
  147.9 69.5 %collective-permute-start.12 = (f32[7,1,8,128]{3,2,1,0:T(8,128)S(1)}, f32[7,1,8,128]{3,2,1,0:T(8,128)S(1)}, u32[]{:S(2)}, u32[]{:S(2)}) collective-permute-start(f32[7,1,8,128]{3,2,1,0:T(8,128)S(1)} %get-tuple-element.32), channel_id=1, source_target_pairs={{0,4},{4,8},{8,12},{12,0},{1,5},{5,9},{9,13},{13,1},{2,6},{6,10},{... | collective-permute-start | bytes 86024 | tf_op jit(solution)/shard_map/ppermute | solution.py:23
  148.0 69.5 %collective-permute-start.13 = (f32[7,1,8,128]{3,2,1,0:T(8,128)S(1)}, f32[7,1,8,128]{3,2,1,0:T(8,128)S(1)}, u32[]{:S(2)}, u32[]{:S(2)}) collective-permute-start(f32[7,1,8,128]{3,2,1,0:T(8,128)S(1)} %get-tuple-element.31), channel_id=1, source_target_pairs={{4,0},{8,4},{12,8},{0,12},{5,1},{9,5},{13,9},{1,13},{6,2},{10,6},{... | collective-permute-start | bytes 86024 | tf_op jit(solution)/shard_map/ppermute | solution.py:24
  151.0 3.6 collective-permute-start.11
  217.4 223.8 %all-reduce.15.cloned.1.call-start = ((), (), s32[]{:S(2)}) async-start(), calls=%async_computation.2 | async-start | bytes 229376 | tf_op jit(solution)/shard_map/psum | solution.py:109
  217.5 4.9 collective-permute-start.15
  220.9 5.6 collective-permute-start.14
  346.0 3.7 collective-permute-start.19
  346.6 3.1 collective-permute-start.18
  346.6 3.1 collective-permute-start.17
  347.1 3.6 collective-permute-start.16
  350.8 3.6 collective-permute-start.20
  352.3 68.6 %collective-permute-start.25 = (f32[7,1,8,128]{3,2,1,0:T(8,128)S(1)}, f32[7,1,8,128]{3,2,1,0:T(8,128)S(1)}, u32[]{:S(2)}, u32[]{:S(2)}) collective-permute-start(f32[7,1,8,128]{3,2,1,0:T(8,128)S(1)} %get-tuple-element.30), channel_id=1, source_target_pairs={{4,0},{8,4},{12,8},{0,12},{5,1},{9,5},{13,9},{1,13},{6,2},{10,6},{... | collective-permute-start | bytes 86024 | tf_op jit(solution)/shard_map/ppermute | solution.py:24
  352.4 68.5 %collective-permute-start.24 = (f32[7,1,8,128]{3,2,1,0:T(8,128)S(1)}, f32[7,1,8,128]{3,2,1,0:T(8,128)S(1)}, u32[]{:S(2)}, u32[]{:S(2)}) collective-permute-start(f32[7,1,8,128]{3,2,1,0:T(8,128)S(1)} %get-tuple-element.29), channel_id=1, source_target_pairs={{0,4},{4,8},{8,12},{12,0},{1,5},{5,9},{9,13},{13,1},{2,6},{6,10},{... | collective-permute-start | bytes 86024 | tf_op jit(solution)/shard_map/ppermute | solution.py:23
  352.8 3.1 collective-permute-start.21
  354.5 3.6 collective-permute-start.23
  420.8 223.4 %all-reduce.17.cloned.1.call-start = ((), (), s32[]{:S(2)}) async-start(), calls=%async_computation.3 | async-start | bytes 229376 | tf_op jit(solution)/shard_map/psum | solution.py:109
  420.9 4.1 collective-permute-start.27
  422.3 5.6 collective-permute-start.26
  549.1 3.7 collective-permute-start.31
  549.7 3.1 collective-permute-start.30
  549.7 3.1 collective-permute-start.29
  550.2 3.6 collective-permute-start.28
  553.9 3.6 collective-permute-start.32
  555.4 68.6 %collective-permute-start.37 = (f32[7,1,8,128]{3,2,1,0:T(8,128)S(1)}, f32[7,1,8,128]{3,2,1,0:T(8,128)S(1)}, u32[]{:S(2)}, u32[]{:S(2)}) collective-permute-start(f32[7,1,8,128]{3,2,1,0:T(8,128)S(1)} %get-tuple-element.28), channel_id=1, source_target_pairs={{4,0},{8,4},{12,8},{0,12},{5,1},{9,5},{13,9},{1,13},{6,2},{10,6},{... | collective-permute-start | bytes 86024 | tf_op jit(solution)/shard_map/ppermute | solution.py:24
  555.4 68.5 %collective-permute-start.36 = (f32[7,1,8,128]{3,2,1,0:T(8,128)S(1)}, f32[7,1,8,128]{3,2,1,0:T(8,128)S(1)}, u32[]{:S(2)}, u32[]{:S(2)}) collective-permute-start(f32[7,1,8,128]{3,2,1,0:T(8,128)S(1)} %get-tuple-element.27), channel_id=1, source_target_pairs={{0,4},{4,8},{8,12},{12,0},{1,5},{5,9},{9,13},{13,1},{2,6},{6,10},{... | collective-permute-start | bytes 86024 | tf_op jit(solution)/shard_map/ppermute | solution.py:23
  555.9 3.1 collective-permute-start.33
  557.5 3.6 collective-permute-start.35
  623.9 223.4 %all-reduce.19.cloned.1.call-start = ((), (), s32[]{:S(2)}) async-start(), calls=%async_computation.4 | async-start | bytes 229376 | tf_op jit(solution)/shard_map/psum | solution.py:109
  624.0 4.1 collective-permute-start.39
  625.4 5.6 collective-permute-start.38
  752.2 3.7 collective-permute-start.43
  753.3 3.6 collective-permute-start.40
  757.0 3.6 collective-permute-start.44
  758.5 68.5 %collective-permute-start.49 = (f32[7,1,8,128]{3,2,1,0:T(8,128)S(1)}, f32[7,1,8,128]{3,2,1,0:T(8,128)S(1)}, u32[]{:S(2)}, u32[]{:S(2)}) collective-permute-start(f32[7,1,8,128]{3,2,1,0:T(8,128)S(1)} %get-tuple-element.26), channel_id=1, source_target_pairs={{4,0},{8,4},{12,8},{0,12},{5,1},{9,5},{13,9},{1,13},{6,2},{10,6},{... | collective-permute-start | bytes 86024 | tf_op jit(solution)/shard_map/ppermute | solution.py:24
  758.5 68.5 %collective-permute-start.48 = (f32[7,1,8,128]{3,2,1,0:T(8,128)S(1)}, f32[7,1,8,128]{3,2,1,0:T(8,128)S(1)}, u32[]{:S(2)}, u32[]{:S(2)}) collective-permute-start(f32[7,1,8,128]{3,2,1,0:T(8,128)S(1)} %get-tuple-element.25), channel_id=1, source_target_pairs={{0,4},{4,8},{8,12},{12,0},{1,5},{5,9},{9,13},{13,1},{2,6},{6,10},{... | collective-permute-start | bytes 86024 | tf_op jit(solution)/shard_map/ppermute | solution.py:23
  759.0 3.1 collective-permute-start.45
  760.6 3.6 collective-permute-start.47
  827.1 4.1 collective-permute-start.51
  828.4 5.6 collective-permute-start.50
  (16 other events, 455.9 us)
Sparse Core Ops, SparseCore 0:
  79.4 22.0 all-reduce.10
  217.5 20.4 all-reduce.12
  421.0 20.1 all-reduce.14
  624.0 20.1 all-reduce.16
  827.2 20.1 all-reduce.18
where the time goes:
time: 893 us; the launch traced here: 892 us
  other arithmetic  335 us (38%)
  blocking collectives  225 us (25%)
  local copies, waits for them, and re-layouts  150 us (17%)
  waiting for transfers between devices  114 us (13%)
  starting transfers between devices  43.1 us (5%)
  between operations  23.6 us (3%)
    scatter-add x5, other arithmetic, spread(): jnp.zeros((species, cell_count), jnp.float32).at[:, cell_places]  253 us
    psum x7, blocking collectives, global_sums(): return lax.psum((terms[0],), ('lon', 'lat'))  225 us
    gather x4, local copies, waits for them, and re-layouts, body(): values = flat_field[:, cells_across]  137 us
    mul x5, other arithmetic, spread(): amounts = (stacked[:, None, :] * lengths_across[None]).reshape(species, -1)  52.9 us
    psum x4, waiting for transfers between devices, body(): summed = lax.psum(partial_image, 'orbit')  51.4 us
    ppermute x36, starting transfers between devices, passed_along(): return lax.ppermute(block, axis, route)  29.1 us
    psum x1, waiting for transfers between devices, body(): rhs_full = lax.psum(spread(ray_source), 'orbit')  22.1 us
    ppermute x36, waiting for transfers between devices, passed_along(): return lax.ppermute(block, axis, route)  20.7 us
  transfers between devices with their start and end apart: 57, of which 35 were waited for; matrix products, arithmetic and copies ran while one was open for 28% of the time, Pallas kernels for 0%

commit v1 on v0

v1 whole, which is shorter than its diff:
```python
import functools

import jax
import jax.numpy as jnp
from jax import lax
from jax.experimental import pallas as pl
from jax.experimental.pallas import tpu as pltpu
from jax.sharding import PartitionSpec as P

CLON = 4
CLAT = 8
LEV = 128
NT = 3
ITERS = 4
SUB = 8
HALF = 256

highest = lax.Precision.HIGHEST
MESH = pl.DeviceIdType.MESH
f32 = jnp.float32
bf16 = jnp.bfloat16
NT_DIMS = (((1,), (1,)), ((), ()))


def each(count, step):
    if count <= 16:
        for k in range(count):
            step(k)
    else:
        lax.fori_loop(0, count, lambda k, c: (step(k), c)[1], 0)


def residues(reach, size):
    found = []
    for d in range(-reach, reach + 1):
        if d % size not in found:
            found.append(d % size)
    found.remove(0)
    return [0] + found


def kernel(sizes, observed, starts, cells, lengths, channel, noise, prior, x_out, r_out,
           ck8, gcol, pw, tab, w_hi, w_lo, latkey, source, ops, lon_halo, lat_halo,
           t_send, t_recv, d_recv, prior_acc, vec_x, vec_r, vec_w, vec_d, vec_s, vec_z,
           source_ssem, source_rsem, tab_ssem, tab_rsem, halo_ssem, halo_rsem,
           t_ssem, t_rsem, d_ssem, d_rsem):
    n_orbit, n_lon, n_lat = sizes
    reach = NT - 1
    span = 2 * NT - 1
    species, channels = channel.shape
    rays = starts.shape[1]
    tile = cells.shape[0]
    groups = residues(reach, n_lon)
    peers = residues(2 * reach, n_lon)
    group_of = [groups.index((u - reach) % n_lon) for u in range(span)]
    planes = n_lon * n_lat
    orbit = lax.axis_index("orbit")
    lon = lax.axis_index("lon")
    lat = lax.axis_index("lat")
    place = lon * n_lat + lat

    barrier = pltpu.get_barrier_semaphore()

    def plane_peer(k):
        there = lax.rem(place + k, planes)
        return (orbit, there // n_lat, lax.rem(there, n_lat))

    def greet(k):
        pl.semaphore_signal(barrier, inc=1, device_id=plane_peer(k + 1), device_id_type=MESH)

    each(planes - 1, greet)
    for o in range(1, n_orbit):
        for d in groups:
            pl.semaphore_signal(
                barrier, inc=1, device_id_type=MESH,
                device_id=(lax.rem(orbit + o, n_orbit), lax.rem(lon + d, n_lon), lat))

    ck8[...] = jnp.zeros_like(ck8)
    ck8[0:species, :] = channel[...]
    kernel_rows = ck8[...]
    weighted = kernel_rows * noise[...]
    gram = lax.dot_general(weighted, kernel_rows, NT_DIMS, precision=highest,
                           preferred_element_type=f32)
    for t in range(species):
        gcol[t] = jnp.broadcast_to(gram[:, t:t + 1], (SUB, LEV))
    sublane = lax.broadcasted_iota(jnp.int32, (SUB, LEV), 0)
    own_source = jnp.dot(weighted, observed[...], precision=highest, preferred_element_type=f32)
    source[orbit, 0] = jnp.where(sublane == species, starts[...].astype(f32), own_source)
    diagonal = (lax.broadcasted_iota(jnp.int32, (SUB, species), 0)
                == lax.broadcasted_iota(jnp.int32, (SUB, species), 1))
    pw_col = jnp.sum(jnp.where(diagonal, prior[...], 0.0), axis=1, keepdims=True)
    pw[...] = jnp.broadcast_to(pw_col, (SUB, LEV))

    own_cells = cells[...]
    own_lengths = lengths[...]
    totals = jnp.zeros_like(own_lengths)
    for m in range(tile):
        totals = totals + jnp.where(own_cells == own_cells[m:m + 1, :], own_lengths[m:m + 1, :], 0.0)
    tab[orbit, 0:tile, :] = own_cells.astype(f32)
    tab[orbit, tile:2 * tile, :] = totals

    pl.semaphore_wait(barrier, planes - 1 + (n_orbit - 1) * len(groups))

    tab_copies = []
    for o in range(1, n_orbit):
        copy = pltpu.make_async_remote_copy(
            src_ref=tab.at[orbit], dst_ref=tab.at[orbit],
            send_sem=tab_ssem.at[o], recv_sem=tab_rsem.at[o],
            device_id=(lax.rem(orbit + o, n_orbit), lon, lat), device_id_type=MESH)
        copy.start()
        tab_copies.append(copy)
    source_copies = []
    for o in range(n_orbit):
        for g, d in enumerate(groups):
            if o == 0 and g == 0:
                continue
            copy = pltpu.make_async_remote_copy(
                src_ref=source.at[orbit, 0], dst_ref=source.at[orbit, g],
                send_sem=source_ssem.at[o, g], recv_sem=source_rsem.at[o, g],
                device_id=(lax.rem(orbit + o, n_orbit), lax.rem(lon + d, n_lon), lat),
                device_id_type=MESH)
            copy.start()
            source_copies.append(copy)

    def build(slot):
        def chunk(c, carry):
            at = pl.ds(pl.multiple_of(c * LEV, LEV), LEV)
            cell = tab[slot, 0:tile, at].astype(jnp.int32)
            key = (cell // (CLAT * LEV)) * LEV + lax.rem(cell, LEV)
            total = tab[slot, tile:2 * tile, at]
            hi = total.astype(bf16).astype(f32)
            lo = total - hi
            rows = (lax.broadcasted_iota(jnp.int32, (HALF // 16, 16, LEV), 0) * 16
                    + lax.broadcasted_iota(jnp.int32, (HALF // 16, 16, LEV), 1))
            rows = rows.astype(f32).astype(bf16)
            for half in range(CLON * LEV // HALF):
                acc_hi = jnp.zeros((HALF // 16, 16, LEV), bf16)
                acc_lo = jnp.zeros((HALF // 16, 16, LEV), bf16)
                near = (key - half * HALF).astype(f32)
                for m in range(tile):
                    wide = lambda v: jnp.broadcast_to(v[m:m + 1, :], (16, LEV)).astype(bf16)[None]
                    hit = rows == wide(near)
                    acc_hi = jnp.where(hit, wide(hi), acc_hi)
                    acc_lo = jnp.where(hit, wide(lo), acc_lo)
                w_hi[slot, half * HALF:(half + 1) * HALF, at] = acc_hi.reshape(HALF, LEV)
                w_lo[slot, half * HALF:(half + 1) * HALF, at] = acc_lo.reshape(HALF, LEV)
            return carry

        lax.fori_loop(0, span * rays // LEV, chunk, 0)

    build(orbit)
    for o in range(1, n_orbit):
        tab_copies[o - 1].wait()
        build(lax.rem(orbit + n_orbit - o, n_orbit))
    for copy in source_copies:
        copy.wait()

    for o in range(n_orbit):
        for u in range(span):
            first = source[o, group_of[u], species:species + 1, :].astype(jnp.int32)
            cell = tab[o, 0:1, u * rays:(u + 1) * rays].astype(jnp.int32)
            band = lax.rem(cell // LEV, CLAT)
            band = jnp.where((first <= u) & (first + reach >= u), band, -1)
            latkey[o, :, u * rays:(u + 1) * rays] = jnp.broadcast_to(band, (SUB, rays))

    def back(images):
        total = None
        for o in range(n_orbit):
            y = jnp.concatenate([images[o][group_of[u]] for u in range(span)], axis=1)
            y_hi = y.astype(bf16).astype(f32)
            y_lo = y - y_hi
            band = latkey[o]
            high = jnp.concatenate([jnp.where(band == b, y_hi, 0.0) for b in range(CLAT)], axis=0)
            low = jnp.concatenate([jnp.where(band == b, y_lo, 0.0) for b in range(CLAT)], axis=0)
            high = high.astype(bf16)
            both = jnp.concatenate([high, low.astype(bf16)], axis=0)
            first = lax.dot_general(both, w_hi[o], NT_DIMS, preferred_element_type=f32)
            second = lax.dot_general(high, w_lo[o], NT_DIMS, preferred_element_type=f32)
            rows = CLAT * SUB
            part = first[0:rows] + (first[rows:] + second)
            total = part if total is None else total + part
        return total

    def product(turn):
        v_ref = ops.at[turn]
        copies = []
        last = (CLON - 1) * LEV
        for side, (src, dst, device) in enumerate((
            (v_ref.at[:, last:last + LEV], lon_halo.at[turn, 0], (orbit, lax.rem(lon + 1, n_lon), lat)),
            (v_ref.at[:, 0:LEV], lon_halo.at[turn, 1], (orbit, lax.rem(lon + n_lon - 1, n_lon), lat)),
            (v_ref.at[(CLAT - 1) * SUB:CLAT * SUB, :], lat_halo.at[turn, 0], (orbit, lon, lax.rem(lat + 1, n_lat))),
            (v_ref.at[0:SUB, :], lat_halo.at[turn, 1], (orbit, lon, lax.rem(lat + n_lat - 1, n_lat))),
        )):
            copy = pltpu.make_async_remote_copy(
                src_ref=src, dst_ref=dst, send_sem=halo_ssem.at[turn, side],
                recv_sem=halo_rsem.at[turn, side], device_id=device, device_id_type=MESH)
            copy.start()
            copies.append(copy)
        v = v_ref[...]
        rows = CLAT * SUB
        v_high = v.astype(bf16)
        v_both = jnp.concatenate([v_high, (v - v_high.astype(f32)).astype(bf16)], axis=0)
        for o in range(n_orbit):
            first = jnp.dot(v_both, w_hi[o], preferred_element_type=f32)
            second = jnp.dot(v_high, w_lo[o], preferred_element_type=f32)
            sums = first[0:rows] + (first[rows:] + second)
            band = latkey[o]
            picked = jnp.zeros((SUB, span * rays), f32)
            for b in range(CLAT):
                picked = jnp.where(band == b, sums[b * SUB:(b + 1) * SUB], picked)
            for g in range(len(groups)):
                mine = [picked[:, u * rays:(u + 1) * rays] for u in range(span) if group_of[u] == g]
                t_send[turn, o * len(groups) + g] = functools.reduce(lambda a, b: a + b, mine)
        t_copies = []
        for k, distance in enumerate(peers):
            if k == 0:
                continue
            copy = pltpu.make_async_remote_copy(
                src_ref=t_send.at[turn], dst_ref=t_recv.at[turn, k - 1],
                send_sem=t_ssem.at[turn, k], recv_sem=t_rsem.at[turn, k],
                device_id=(orbit, lax.rem(lon + distance, n_lon), lat), device_id_type=MESH)
            copy.start()
            t_copies.append(copy)

        for copy in copies:
            copy.wait()
        lane = lax.broadcasted_iota(jnp.int32, (rows, LEV), 1)
        weight = jnp.concatenate([pw[...]] * CLAT, axis=0)
        column = lambda c: v_ref[:, c * LEV:(c + 1) * LEV]
        for c in range(CLON):
            here = column(c)
            south = jnp.where(lat == 0, 0.0, lat_halo[turn, 0, :, c * LEV:(c + 1) * LEV])
            north = jnp.where(lat == n_lat - 1, 0.0, lat_halo[turn, 1, :, c * LEV:(c + 1) * LEV])
            around = column(c - 1) if c > 0 else lon_halo[turn, 0]
            around = around + (column(c + 1) if c < CLON - 1 else lon_halo[turn, 1])
            around = around + jnp.concatenate([south, here[:-SUB]], axis=0)
            around = around + jnp.concatenate([here[SUB:], north], axis=0)
            around = around + jnp.where(lane == 0, 0.0, pltpu.roll(here, 1, 1))
            around = around + jnp.where(lane == LEV - 1, 0.0, pltpu.roll(here, LEV - 1, 1))
            prior_acc[:, c * LEV:(c + 1) * LEV] = weight * (6.0 * here - around)

        for copy in t_copies:
            copy.wait()
        images = []
        for o in range(n_orbit):
            per_group = []
            for g, d in enumerate(groups):
                total = t_send[turn, o * len(groups) + g]
                for k, distance in enumerate(peers):
                    theirs = (d - distance) % n_lon
                    if k > 0 and theirs in groups:
                        total = total + t_recv[turn, k - 1, o * len(groups) + groups.index(theirs)]
                image = jnp.zeros((SUB, rays), f32)
                for t in range(species):
                    image = image + gcol[t] * total[t:t + 1, :]
                per_group.append(image)
            images.append(per_group)
        return back(images) + prior_acc[...]

    def inner(a, b):
        whole = a * b
        lanes = sum(whole[:, c * LEV:(c + 1) * LEV] for c in range(CLON))
        return jnp.sum(lanes, axis=0, keepdims=True)

    def start_dots(turn):
        r = vec_r[...]
        w = vec_w[...]
        terms = [inner(r, r), inner(r, w)]
        if turn > 0:
            terms += [inner(r, vec_s[...]), inner(vec_d[...], w)]
        terms.append(jnp.zeros((SUB - len(terms), LEV), f32))
        d_recv[turn, 0] = jnp.concatenate(terms, axis=0)

        def send(k):
            pltpu.make_async_remote_copy(
                src_ref=d_recv.at[turn, 0], dst_ref=d_recv.at[turn, k + 1],
                send_sem=d_ssem.at[turn], recv_sem=d_rsem.at[turn],
                device_id=plane_peer(k + 1), device_id_type=MESH).start()

        each(planes - 1, send)

    def finish_dots(turn):
        pltpu.make_async_remote_copy(
            src_ref=d_recv.at[turn, pl.ds(1, planes - 1)], dst_ref=d_recv.at[turn, pl.ds(1, planes - 1)],
            send_sem=d_ssem.at[turn], recv_sem=d_rsem.at[turn],
            device_id=plane_peer(1), device_id_type=MESH).wait()
        total = jnp.zeros((SUB, LEV), f32)
        for f in range(planes):
            total = total + d_recv[turn, lax.rem(place + planes - f, planes)]
        sums = jnp.sum(total, axis=1, keepdims=True)
        return [sums[i:i + 1, :] for i in range(4)]

    images = [[jnp.where(sublane < species, source[o, g], 0.0) for g in range(len(groups))]
              for o in range(n_orbit)]
    right_side = back(images)
    vec_r[...] = right_side
    ops[0] = right_side
    vec_w[...] = product(0)
    norm_before = None
    curvature = None
    for turn in range(ITERS):
        start_dots(turn)
        more = turn < ITERS - 1
        if more:
            ops[turn + 1] = vec_w[...]
            image = product(turn + 1)
        norm, cross, cross_s, cross_d = finish_dots(turn)
        if turn == 0:
            curvature = cross
            alpha = norm / curvature
            direction = vec_r[...]
            moved = vec_w[...]
            vec_x[...] = alpha * direction
            if more:
                twice = image
        else:
            beta = norm / norm_before
            curvature = cross + beta * (cross_s + cross_d) + beta * beta * curvature
            alpha = norm / curvature
            direction = vec_r[...] + beta * vec_d[...]
            moved = vec_w[...] + beta * vec_s[...]
            vec_x[...] = vec_x[...] + alpha * direction
            if more:
                twice = image + beta * vec_z[...]
        vec_r[...] = vec_r[...] - alpha * moved
        if more:
            vec_d[...] = direction
            vec_s[...] = moved
            vec_z[...] = twice
            vec_w[...] = vec_w[...] - alpha * twice
        norm_before = norm
    x_out[...] = vec_x[...]
    r_out[...] = vec_r[...]


def body(sizes, observed, ray_start, tile_cells, tile_lengths, channel_kernel, noise_weight, prior_weight):
    n_orbit, n_lon, n_lat = sizes
    species, channels = channel_kernel.shape
    rays = ray_start.shape[0]
    rows, tile = tile_cells.shape
    groups = len(residues(NT - 1, n_lon))
    peers = len(residues(2 * (NT - 1), n_lon))
    flat = (CLAT * SUB, CLON * LEV)
    vmem = pltpu.VMEM
    dma = pltpu.SemaphoreType.DMA
    out = jax.ShapeDtypeStruct(flat, f32)
    solved, left = pl.pallas_call(
        functools.partial(kernel, sizes),
        out_shape=(out, out),
        in_specs=[pl.BlockSpec(memory_space=pltpu.VMEM)] * 7,
        out_specs=[pl.BlockSpec(memory_space=pltpu.VMEM)] * 2,
        scratch_shapes=[
            vmem((SUB, channels), f32),
            vmem((species, SUB, LEV), f32),
            vmem((SUB, LEV), f32),
            vmem((n_orbit, 2 * tile, rows), f32),
            vmem((n_orbit, CLON * LEV, rows), bf16),
            vmem((n_orbit, CLON * LEV, rows), bf16),
            vmem((n_orbit, SUB, rows), jnp.int32),
            vmem((n_orbit, groups, SUB, rays), f32),
            vmem((ITERS,) + flat, f32),
            vmem((ITERS, 2, flat[0], LEV), f32),
            vmem((ITERS, 2, SUB, flat[1]), f32),
            vmem((ITERS, n_orbit * groups, SUB, rays), f32),
            vmem((ITERS, peers - 1, n_orbit * groups, SUB, rays), f32),
            vmem((ITERS, n_lon * n_lat, SUB, LEV), f32),
        ] + [vmem(flat, f32)] * 7 + [
            dma((n_orbit, groups)), dma((n_orbit, groups)),
            dma((n_orbit,)), dma((n_orbit,)),
            dma((ITERS, 4)), dma((ITERS, 4)),
            dma((ITERS, peers)), dma((ITERS, peers)),
            dma((ITERS,)), dma((ITERS,)),
        ],
        compiler_params=pltpu.CompilerParams(
            collective_id=0, has_side_effects=True, vmem_limit_bytes=40 * 1024 * 1024),
    )(
        observed.T, ray_start.reshape(1, rays), tile_cells.T, tile_lengths.T,
        channel_kernel, noise_weight.reshape(1, channels), prior_weight.reshape(1, species),
    )

    def placed(field):
        shaped = field.reshape(CLAT, SUB, CLON, LEV)[:, :species]
        return shaped.transpose(1, 2, 0, 3)

    return placed(solved), placed(left)


def solution(mesh):
    sizes = tuple(mesh.shape[name] for name in ("orbit", "lon", "lat"))
    return jax.shard_map(
        functools.partial(body, sizes),
        mesh=mesh,
        in_specs=(
            P(("orbit", "lon", "lat"), None),
            P(("orbit", "lon", "lat")),
            P(("orbit", "lon", "lat"), None),
            P(("orbit", "lon", "lat"), None),
            P(),
            P(),
            P(),
        ),
        out_specs=(P(None, "lon", "lat", None), P(None, "lon", "lat", None)),
        check_vma=False,
    )
```

time: 893 us -> 44.7 us (0.05)
  other arithmetic: 335 us -> 0 us
  blocking collectives: 225 us -> 0 us
  local copies, waits for them, and re-layouts: 150 us -> 3.8 us
  waiting for transfers between devices: 114 us -> 0 us
  starting transfers between devices: 43.1 us -> 0 us
  Pallas kernels: 0 us -> 39.8 us
  between operations: 23.6 us -> 0.68 us
    scatter-add x5 -> x0, other arithmetic: 253 us -> none  [spread(): jnp.zeros((species, cell_count), jnp.float32).at[:, cell_places]]
    psum x7 -> x0, blocking collectives: 225 us -> none  [global_sums(): return lax.psum((terms[0],), ('lon', 'lat'))]
    gather x4 -> x0, local copies, waits for them, and re-layouts: 137 us -> none  [body(): values = flat_field[:, cells_across]]
    psum x5 -> x0, waiting for transfers between devices: 73.5 us -> none  [the longest x4 51.4 us: body(): summed = lax.psum(partial_image, 'orbit')]
    mul x5 -> x0, other arithmetic: 52.9 us -> none  [spread(): amounts = (stacked[:, None, :] * lengths_across[None]).reshape(species, -1)]
    ppermute x52 -> x0, starting transfers between devices: 42.9 us -> none  [the longest x36 29.1 us: passed_along(): return lax.ppermute(block, axis, route)]
    ppermute x52 -> x0, waiting for transfers between devices: 40 us -> none  [the longest x36 20.7 us: passed_along(): return lax.ppermute(block, axis, route)]
    pallas_call x0 -> x1, Pallas kernels: none -> 39.8 us  [body(): pl.pallas_call(functools.partial(kernel, sizes), out_shape=(out, out), in...]
  transfers between devices with their start and end apart: 57 -> 0, of which waited for: 35 -> 0; matrix products, arithmetic and copies ran while one was open for 28% -> 0% of each run, Pallas kernels for 0% -> 0%
where the time goes in v1:
time: 44.7 us; the launch traced here: 44.3 us
  Pallas kernels  39.8 us (89%)
  local copies, waits for them, and re-layouts  3.8 us (9%)
  between operations  0.68 us (2%)
    pallas_call x1, Pallas kernels, body(): pl.pallas_call(functools.partial(kernel, sizes), out_shape=(out, out), in...  39.8 us
    unnamed x14, local copies, waits for them, and re-layouts  2.98 us

profile of v1, /device:TPU:0, one launch (start us, length us, event | category | flops | bytes accessed | tf_op | source)
XLA Modules:
  0.0 44.3 jit_solution(8018568602586772035)
XLA Ops:
  0.6 0.0 copy-start.3
  0.6 0.0 copy-start.4
  0.7 0.0 copy-start.5
  0.7 0.0 copy-start.6
  0.7 0.6 %copy-done.3 = f32[7,64]{1,0:T(8,128)S(1)} copy-done((f32[7,64]{1,0:T(8,128)S(1)}, f32[7,64]{1,0:T(8,128)}, u32[]{:S(2)}) %copy-start.3) | copy-done | bytes 1816
  1.3 0.0 copy-done.4
  1.3 0.0 copy-done.5
  1.3 0.0 copy-done.6
  1.3 0.0 copy-start
  1.3 0.8 %copy-done = s32[640,16]{0,1:T(8,128)S(1)} copy-done((s32[640,16]{0,1:T(8,128)S(1)}, s32[640,16]{0,1:T(8,128)}, u32[]{:S(2)}) %copy-start) | copy-done | bytes 40984
  2.1 0.0 copy-start.1
  2.1 0.8 %copy-done.1 = f32[640,16]{0,1:T(8,128)S(1)} copy-done((f32[640,16]{0,1:T(8,128)S(1)}, f32[640,16]{0,1:T(8,128)}, u32[]{:S(2)}) %copy-start.1) | copy-done | bytes 40984
  2.9 0.0 copy-start.2
  2.9 0.8 %copy-done.2 = f32[128,64]{0,1:T(8,128)S(1)} copy-done((f32[128,64]{0,1:T(8,128)S(1)}, f32[128,64]{0,1:T(8,128)}, u32[]{:S(2)}) %copy-start.2) | copy-done | bytes 32792
  3.7 39.8 %shard_map.86 = (f32[64,512]{1,0:T(8,128)S(1)}, f32[64,512]{1,0:T(8,128)S(1)}) custom-call(f32[64,128]{1,0:T(8,128)S(1)} %bitcast.18, s32[1,128]{1,0:T(1,128)S(1)} %bitcast.19, s32[16,640]{1,0:T(8,128)S(1)} %bitcast.16, f32[16,640]{1,0:T(8,128)S(1)} %bitcast.17, f32[7,64]{1,0:T(8,128)S(1)} %copy-done.3, f32[1,64]{1,0:T(1,128)S(1)} %bitcast.20, ...), custom_call_target="tpu_custom_call" | custom-call | tf_op jit(solution)/shard_map/pallas_call | solution.py:347
  43.5 0.8 %copy_bitcast_fusion = (f32[7,4,8,128]{3,2,1,0:T(8,128)}, f32[7,4,8,128]{3,2,1,0:T(8,128)}) fusion(f32[8,7,4,128]{3,1,2,0:T(8,128)S(1)} %bitcast.15, f32[8,7,4,128]{3,1,2,0:T(8,128)S(1)} %bitcast.14), kind=kLoop, calls=%fused_computation | loop fusion | bytes 458752 | tf_op jit(solution)/shard_map/transpose | solution.py:383
Async XLA Ops:
  0.6 0.7 %copy-start.3 = (f32[7,64]{1,0:T(8,128)S(1)}, f32[7,64]{1,0:T(8,128)}, u32[]{:S(2)}) copy-start(f32[7,64]{1,0:T(8,128)} %channel.1) | copy-start | bytes 5380
  0.6 0.7 %copy-start.4 = (s32[128]{0:T(128)S(1)}, s32[128]{0:T(128)}, u32[]{:S(2)}) copy-start(s32[128]{0:T(128)} %param.8) | copy-start | bytes 1540
  0.7 0.7 %copy-start.5 = (f32[64]{0:T(128)S(1)}, f32[64]{0:T(128)}, u32[]{:S(2)}) copy-start(f32[64]{0:T(128)} %param.12) | copy-start | bytes 772
  0.7 0.7 %copy-start.6 = (f32[7]{0:T(128)S(1)}, f32[7]{0:T(128)}, u32[]{:S(2)}) copy-start(f32[7]{0:T(128)} %param.13) | copy-start | bytes 88
  1.3 0.8 %copy-start = (s32[640,16]{0,1:T(8,128)S(1)}, s32[640,16]{0,1:T(8,128)}, u32[]{:S(2)}) copy-start(s32[640,16]{0,1:T(8,128)} %param.9) | copy-start | bytes 122884
  2.1 0.8 %copy-start.1 = (f32[640,16]{0,1:T(8,128)S(1)}, f32[640,16]{0,1:T(8,128)}, u32[]{:S(2)}) copy-start(f32[640,16]{0,1:T(8,128)} %param.10) | copy-start | bytes 122884
  2.9 0.8 %copy-start.2 = (f32[128,64]{0,1:T(8,128)S(1)}, f32[128,64]{0,1:T(8,128)}, u32[]{:S(2)}) copy-start(f32[128,64]{0,1:T(8,128)} %param.7) | copy-start | bytes 98308

commit v2 on v1

--- a/solution.py
+++ b/solution.py
@@ -39,7 +39,8 @@
     return [0] + found
 
 
-def kernel(sizes, observed, starts, cells, lengths, channel, noise, prior, x_out, r_out,
+def kernel(sizes, observed_in, starts_in, cells_in, lengths_in, channel_in, noise_in, prior_in,
+           x_out, r_out, observed, starts, cells, lengths, channel, noise, prior, load_sem,
            ck8, gcol, pw, tab, w_hi, w_lo, latkey, source, ops, lon_halo, lat_halo,
            t_send, t_recv, d_recv, prior_acc, vec_x, vec_r, vec_w, vec_d, vec_s, vec_z,
            source_ssem, source_rsem, tab_ssem, tab_rsem, halo_ssem, halo_rsem,
@@ -60,10 +61,18 @@
     place = lon * n_lat + lat
 
     barrier = pltpu.get_barrier_semaphore()
+    loads = [
+        pltpu.make_async_copy(src, dst, load_sem.at[i])
+        for i, (src, dst) in enumerate((
+            (cells_in, cells), (lengths_in, lengths), (observed_in, observed), (channel_in, channel),
+            (noise_in, noise), (starts_in, starts), (prior_in, prior)))
+    ]
+    for load in loads:
+        load.start()
 
     def plane_peer(k):
         there = lax.rem(place + k, planes)
-        return (orbit, there // n_lat, lax.rem(there, n_lat))
+        return (orbit, lax.div(there, n_lat), lax.rem(there, n_lat))
 
     def greet(k):
         pl.semaphore_signal(barrier, inc=1, device_id=plane_peer(k + 1), device_id_type=MESH)
@@ -75,22 +84,8 @@
                 barrier, inc=1, device_id_type=MESH,
                 device_id=(lax.rem(orbit + o, n_orbit), lax.rem(lon + d, n_lon), lat))
 
-    ck8[...] = jnp.zeros_like(ck8)
-    ck8[0:species, :] = channel[...]
-    kernel_rows = ck8[...]
-    weighted = kernel_rows * noise[...]
-    gram = lax.dot_general(weighted, kernel_rows, NT_DIMS, precision=highest,
-                           preferred_element_type=f32)
-    for t in range(species):
-        gcol[t] = jnp.broadcast_to(gram[:, t:t + 1], (SUB, LEV))
-    sublane = lax.broadcasted_iota(jnp.int32, (SUB, LEV), 0)
-    own_source = jnp.dot(weighted, observed[...], precision=highest, preferred_element_type=f32)
-    source[orbit, 0] = jnp.where(sublane == species, starts[...].astype(f32), own_source)
-    diagonal = (lax.broadcasted_iota(jnp.int32, (SUB, species), 0)
-                == lax.broadcasted_iota(jnp.int32, (SUB, species), 1))
-    pw_col = jnp.sum(jnp.where(diagonal, prior[...], 0.0), axis=1, keepdims=True)
-    pw[...] = jnp.broadcast_to(pw_col, (SUB, LEV))
-
+    for load in loads[:2]:
+        load.wait()
     own_cells = cells[...]
     own_lengths = lengths[...]
     totals = jnp.zeros_like(own_lengths)
@@ -109,6 +104,15 @@
             device_id=(lax.rem(orbit + o, n_orbit), lon, lat), device_id_type=MESH)
         copy.start()
         tab_copies.append(copy)
+    for load in loads[2:]:
+        load.wait()
+    ck8[...] = jnp.zeros_like(ck8)
+    ck8[0:species, :] = channel[...]
+    kernel_rows = ck8[...]
+    weighted = kernel_rows * noise[...]
+    sublane = lax.broadcasted_iota(jnp.int32, (SUB, LEV), 0)
+    own_source = jnp.dot(weighted, observed[...], precision=highest, preferred_element_type=f32)
+    source[orbit, 0] = jnp.where(sublane == species, starts[...].astype(f32), own_source)
     source_copies = []
     for o in range(n_orbit):
         for g, d in enumerate(groups):
@@ -121,6 +125,15 @@
                 device_id_type=MESH)
             copy.start()
             source_copies.append(copy)
+
+    gram = lax.dot_general(weighted, kernel_rows, NT_DIMS, precision=highest,
+                           preferred_element_type=f32)
+    for t in range(species):
+        gcol[t] = jnp.broadcast_to(gram[:, t:t + 1], (SUB, LEV))
+    diagonal = (lax.broadcasted_iota(jnp.int32, (SUB, species), 0)
+                == lax.broadcasted_iota(jnp.int32, (SUB, species), 1))
+    pw_col = jnp.sum(jnp.where(diagonal, prior[...], 0.0), axis=1, keepdims=True)
+    pw[...] = jnp.broadcast_to(pw_col, (SUB, LEV))
 
     def build(slot):
         def chunk(c, carry):
@@ -166,22 +179,25 @@
     def back(images):
         total = None
         for o in range(n_orbit):
-            y = jnp.concatenate([images[o][group_of[u]] for u in range(span)], axis=1)
-            y_hi = y.astype(bf16).astype(f32)
-            y_lo = y - y_hi
-            band = latkey[o]
-            high = jnp.concatenate([jnp.where(band == b, y_hi, 0.0) for b in range(CLAT)], axis=0)
-            low = jnp.concatenate([jnp.where(band == b, y_lo, 0.0) for b in range(CLAT)], axis=0)
-            high = high.astype(bf16)
-            both = jnp.concatenate([high, low.astype(bf16)], axis=0)
-            first = lax.dot_general(both, w_hi[o], NT_DIMS, preferred_element_type=f32)
-            second = lax.dot_general(high, w_lo[o], NT_DIMS, preferred_element_type=f32)
-            rows = CLAT * SUB
-            part = first[0:rows] + (first[rows:] + second)
+            part = back_orbit(o, images[o])
             total = part if total is None else total + part
         return total
 
-    def product(turn):
+    def back_orbit(o, per_group):
+        y = jnp.concatenate([per_group[group_of[u]] for u in range(span)], axis=1)
+        y_hi = y.astype(bf16).astype(f32)
+        y_lo = y - y_hi
+        band = latkey[o]
+        high = jnp.concatenate([jnp.where(band == b, y_hi, 0.0) for b in range(CLAT)], axis=0)
+        low = jnp.concatenate([jnp.where(band == b, y_lo, 0.0) for b in range(CLAT)], axis=0)
+        high = high.astype(bf16)
+        both = jnp.concatenate([high, low.astype(bf16)], axis=0)
+        first = lax.dot_general(both, w_hi[o], NT_DIMS, preferred_element_type=f32)
+        second = lax.dot_general(high, w_lo[o], NT_DIMS, preferred_element_type=f32)
+        rows = CLAT * SUB
+        return first[0:rows] + (first[rows:] + second)
+
+    def product(turn, send_sums=None, between=None):
         v_ref = ops.at[turn]
         copies = []
         last = (CLON - 1) * LEV
@@ -199,6 +215,7 @@
         v = v_ref[...]
         rows = CLAT * SUB
         v_high = v.astype(bf16)
+        t_copies = [[] for _ in range(n_orbit)]
         v_both = jnp.concatenate([v_high, (v - v_high.astype(f32)).astype(bf16)], axis=0)
         for o in range(n_orbit):
             first = jnp.dot(v_both, w_hi[o], preferred_element_type=f32)
@@ -210,17 +227,18 @@
                 picked = jnp.where(band == b, sums[b * SUB:(b + 1) * SUB], picked)
             for g in range(len(groups)):
                 mine = [picked[:, u * rays:(u + 1) * rays] for u in range(span) if group_of[u] == g]
-                t_send[turn, o * len(groups) + g] = functools.reduce(lambda a, b: a + b, mine)
-        t_copies = []
-        for k, distance in enumerate(peers):
-            if k == 0:
-                continue
-            copy = pltpu.make_async_remote_copy(
-                src_ref=t_send.at[turn], dst_ref=t_recv.at[turn, k - 1],
-                send_sem=t_ssem.at[turn, k], recv_sem=t_rsem.at[turn, k],
-                device_id=(orbit, lax.rem(lon + distance, n_lon), lat), device_id_type=MESH)
-            copy.start()
-            t_copies.append(copy)
+                t_send[turn, o, g] = functools.reduce(lambda a, b: a + b, mine)
+            for k, distance in enumerate(peers):
+                if k == 0:
+                    continue
+                copy = pltpu.make_async_remote_copy(
+                    src_ref=t_send.at[turn, o], dst_ref=t_recv.at[turn, k - 1, o],
+                    send_sem=t_ssem.at[turn, k, o], recv_sem=t_rsem.at[turn, k, o],
+                    device_id=(orbit, lax.rem(lon + distance, n_lon), lat), device_id_type=MESH)
+                copy.start()
+                t_copies[o].append(copy)
+            if o == 0 and send_sums is not None:
+                send_sums()
 
         for copy in copies:
             copy.wait()
@@ -239,38 +257,44 @@
             around = around + jnp.where(lane == LEV - 1, 0.0, pltpu.roll(here, LEV - 1, 1))
             prior_acc[:, c * LEV:(c + 1) * LEV] = weight * (6.0 * here - around)
 
-        for copy in t_copies:
-            copy.wait()
-        images = []
+        if between is not None:
+            between()
+        result = prior_acc[...]
         for o in range(n_orbit):
+            for copy in t_copies[o]:
+                copy.wait()
             per_group = []
             for g, d in enumerate(groups):
-                total = t_send[turn, o * len(groups) + g]
+                total = t_send[turn, o, g]
                 for k, distance in enumerate(peers):
                     theirs = (d - distance) % n_lon
                     if k > 0 and theirs in groups:
-                        total = total + t_recv[turn, k - 1, o * len(groups) + groups.index(theirs)]
+                        total = total + t_recv[turn, k - 1, o, groups.index(theirs)]
                 image = jnp.zeros((SUB, rays), f32)
                 for t in range(species):
                     image = image + gcol[t] * total[t:t + 1, :]
                 per_group.append(image)
-            images.append(per_group)
-        return back(images) + prior_acc[...]
+            result = result + back_orbit(o, per_group)
+        return result
 
     def inner(a, b):
         whole = a * b
         lanes = sum(whole[:, c * LEV:(c + 1) * LEV] for c in range(CLON))
-        return jnp.sum(lanes, axis=0, keepdims=True)
-
-    def start_dots(turn):
+        return jnp.sum(jnp.sum(lanes, axis=0, keepdims=True), axis=1, keepdims=True)
+
+    def form_dots(turn):
         r = vec_r[...]
-        w = vec_w[...]
+        w = ops[turn + 1] if turn + 1 < ITERS else vec_w[...]
         terms = [inner(r, r), inner(r, w)]
         if turn > 0:
             terms += [inner(r, vec_s[...]), inner(vec_d[...], w)]
-        terms.append(jnp.zeros((SUB - len(terms), LEV), f32))
-        d_recv[turn, 0] = jnp.concatenate(terms, axis=0)
-
+        spot = lax.broadcasted_iota(jnp.int32, (1, LEV), 1)
+        row = jnp.zeros((1, LEV), f32)
+        for i, term in enumerate(terms):
+            row = jnp.where(spot == i, term, row)
+        d_recv[turn, 0] = row
+
+    def send_dots(turn):
         def send(k):
             pltpu.make_async_remote_copy(
                 src_ref=d_recv.at[turn, 0], dst_ref=d_recv.at[turn, k + 1],
@@ -284,51 +308,56 @@
             src_ref=d_recv.at[turn, pl.ds(1, planes - 1)], dst_ref=d_recv.at[turn, pl.ds(1, planes - 1)],
             send_sem=d_ssem.at[turn], recv_sem=d_rsem.at[turn],
             device_id=plane_peer(1), device_id_type=MESH).wait()
-        total = jnp.zeros((SUB, LEV), f32)
+        total = jnp.zeros((1, LEV), f32)
         for f in range(planes):
             total = total + d_recv[turn, lax.rem(place + planes - f, planes)]
-        sums = jnp.sum(total, axis=1, keepdims=True)
-        return [sums[i:i + 1, :] for i in range(4)]
+        return [total[:, i:i + 1] for i in range(4)]
 
     images = [[jnp.where(sublane < species, source[o, g], 0.0) for g in range(len(groups))]
               for o in range(n_orbit)]
     right_side = back(images)
     vec_r[...] = right_side
     ops[0] = right_side
-    vec_w[...] = product(0)
-    norm_before = None
-    curvature = None
-    for turn in range(ITERS):
-        start_dots(turn)
-        more = turn < ITERS - 1
-        if more:
-            ops[turn + 1] = vec_w[...]
-            image = product(turn + 1)
+    ops[1] = product(0)
+    kept = {}
+
+    def advance(turn):
         norm, cross, cross_s, cross_d = finish_dots(turn)
+        w = ops[turn + 1] if turn + 1 < ITERS else vec_w[...]
         if turn == 0:
-            curvature = cross
-            alpha = norm / curvature
+            kept["curvature"] = cross
+            alpha = norm / cross
             direction = vec_r[...]
-            moved = vec_w[...]
+            moved = w
             vec_x[...] = alpha * direction
-            if more:
-                twice = image
         else:
-            beta = norm / norm_before
-            curvature = cross + beta * (cross_s + cross_d) + beta * beta * curvature
-            alpha = norm / curvature
+            beta = norm / kept["norm"]
+            kept["beta"] = beta
+            kept["curvature"] = cross + beta * (cross_s + cross_d) + beta * beta * kept["curvature"]
+            alpha = norm / kept["curvature"]
             direction = vec_r[...] + beta * vec_d[...]
-            moved = vec_w[...] + beta * vec_s[...]
+            moved = w + beta * vec_s[...]
             vec_x[...] = vec_x[...] + alpha * direction
-            if more:
-                twice = image + beta * vec_z[...]
         vec_r[...] = vec_r[...] - alpha * moved
-        if more:
+        if turn < ITERS - 1:
             vec_d[...] = direction
             vec_s[...] = moved
-            vec_z[...] = twice
-            vec_w[...] = vec_w[...] - alpha * twice
-        norm_before = norm
+        kept["norm"] = norm
+        kept["alpha"] = alpha
+
+    for turn in range(ITERS - 1):
+        form_dots(turn)
+        image = product(turn + 1, lambda: send_dots(turn), lambda: advance(turn))
+        twice = image if turn == 0 else image + kept["beta"] * vec_z[...]
+        vec_z[...] = twice
+        moved_on = ops[turn + 1] - kept["alpha"] * twice
+        if turn + 2 < ITERS:
+            ops[turn + 2] = moved_on
+        else:
+            vec_w[...] = moved_on
+    form_dots(ITERS - 1)
+    send_dots(ITERS - 1)
+    advance(ITERS - 1)
     x_out[...] = vec_x[...]
     r_out[...] = vec_r[...]
 
@@ -347,9 +376,17 @@
     solved, left = pl.pallas_call(
         functools.partial(kernel, sizes),
         out_shape=(out, out),
-        in_specs=[pl.BlockSpec(memory_space=pltpu.VMEM)] * 7,
+        in_specs=[pl.BlockSpec(memory_space=pltpu.HBM)] * 7,
         out_specs=[pl.BlockSpec(memory_space=pltpu.VMEM)] * 2,
         scratch_shapes=[
+            vmem((channels, rays), f32),
+            vmem((1, rays), jnp.int32),
+            vmem((tile, rows), jnp.int32),
+            vmem((tile, rows), f32),
+            vmem((species, channels), f32),
+            vmem((1, channels), f32),
+            vmem((1, species), f32),
+            dma((7,)),
             vmem((SUB, channels), f32),
             vmem((species, SUB, LEV), f32),
             vmem((SUB, LEV), f32),
@@ -361,14 +398,14 @@
             vmem((ITERS,) + flat, f32),
             vmem((ITERS, 2, flat[0], LEV), f32),
             vmem((ITERS, 2, SUB, flat[1]), f32),
-            vmem((ITERS, n_orbit * groups, SUB, rays), f32),
-            vmem((ITERS, peers - 1, n_orbit * groups, SUB, rays), f32),
-            vmem((ITERS, n_lon * n_lat, SUB, LEV), f32),
+            vmem((ITERS, n_orbit, groups, SUB, rays), f32),
+            vmem((ITERS, peers - 1, n_orbit, groups, SUB, rays), f32),
+            vmem((ITERS, n_lon * n_lat, 1, LEV), f32),
         ] + [vmem(flat, f32)] * 7 + [
             dma((n_orbit, groups)), dma((n_orbit, groups)),
             dma((n_orbit,)), dma((n_orbit,)),
             dma((ITERS, 4)), dma((ITERS, 4)),
-            dma((ITERS, peers)), dma((ITERS, peers)),
+            dma((ITERS, peers, n_orbit)), dma((ITERS, peers, n_orbit)),
             dma((ITERS,)), dma((ITERS,)),
         ],
         compiler_params=pltpu.CompilerParams(

time: 44.7 us -> 44.8 us (level)
  no operation moved by 1% of the time
where the time goes in v2:
time: 44.8 us; the launch traced here: 44.5 us
  Pallas kernels  40 us (89%)
  local copies, waits for them, and re-layouts  3.8 us (8%)
  between operations  0.68 us (2%)
    pallas_call x1, Pallas kernels, body(): pl.pallas_call(functools.partial(kernel, sizes), out_shape=(out, out), in...  40 us
    unnamed x14, local copies, waits for them, and re-layouts  2.98 us

profile of v2, /device:TPU:0, one launch (start us, length us, event | category | flops | bytes accessed | tf_op | source)
XLA Modules:
  0.0 44.5 jit_solution(6344933889805955327)
XLA Ops:
  0.6 0.0 copy-start.3
  0.6 0.0 copy-start.4
  0.7 0.0 copy-start.5
  0.7 0.0 copy-start.6
  0.7 0.6 %copy-done.3 = f32[7,64]{1,0:T(8,128)S(1)} copy-done((f32[7,64]{1,0:T(8,128)S(1)}, f32[7,64]{1,0:T(8,128)}, u32[]{:S(2)}) %copy-start.3) | copy-done | bytes 1816
  1.3 0.0 copy-done.4
  1.3 0.0 copy-done.5
  1.3 0.0 copy-done.6
  1.3 0.0 copy-start
  1.3 0.8 %copy-done = s32[640,16]{0,1:T(8,128)S(1)} copy-done((s32[640,16]{0,1:T(8,128)S(1)}, s32[640,16]{0,1:T(8,128)}, u32[]{:S(2)}) %copy-start) | copy-done | bytes 40984
  2.1 0.0 copy-start.1
  2.1 0.8 %copy-done.1 = f32[640,16]{0,1:T(8,128)S(1)} copy-done((f32[640,16]{0,1:T(8,128)S(1)}, f32[640,16]{0,1:T(8,128)}, u32[]{:S(2)}) %copy-start.1) | copy-done | bytes 40984
  2.9 0.0 copy-start.2
  2.9 0.8 %copy-done.2 = f32[128,64]{0,1:T(8,128)S(1)} copy-done((f32[128,64]{0,1:T(8,128)S(1)}, f32[128,64]{0,1:T(8,128)}, u32[]{:S(2)}) %copy-start.2) | copy-done | bytes 32792
  3.7 40.0 %shard_map.86 = (f32[64,512]{1,0:T(8,128)S(1)}, f32[64,512]{1,0:T(8,128)S(1)}) custom-call(f32[64,128]{1,0:T(8,128)S(1)} %bitcast.18, s32[1,128]{1,0:T(1,128)S(1)} %bitcast.19, s32[16,640]{1,0:T(8,128)S(1)} %bitcast.16, f32[16,640]{1,0:T(8,128)S(1)} %bitcast.17, f32[7,64]{1,0:T(8,128)S(1)} %copy-done.3, f32[1,64]{1,0:T(1,128)S(1)} %bitcast.20, ...), custom_call_target="tpu_custom_call" | custom-call | tf_op jit(solution)/shard_map/pallas_call | solution.py:376
  43.7 0.8 %copy_bitcast_fusion = (f32[7,4,8,128]{3,2,1,0:T(8,128)}, f32[7,4,8,128]{3,2,1,0:T(8,128)}) fusion(f32[8,7,4,128]{3,1,2,0:T(8,128)S(1)} %bitcast.15, f32[8,7,4,128]{3,1,2,0:T(8,128)S(1)} %bitcast.14), kind=kLoop, calls=%fused_computation | loop fusion | bytes 458752 | tf_op jit(solution)/shard_map/transpose | solution.py:420
Async XLA Ops:
  0.6 0.7 %copy-start.3 = (f32[7,64]{1,0:T(8,128)S(1)}, f32[7,64]{1,0:T(8,128)}, u32[]{:S(2)}) copy-start(f32[7,64]{1,0:T(8,128)} %channel_in.1) | copy-start | bytes 5380
  0.6 0.7 %copy-start.4 = (s32[128]{0:T(128)S(1)}, s32[128]{0:T(128)}, u32[]{:S(2)}) copy-start(s32[128]{0:T(128)} %param.8) | copy-start | bytes 1540
  0.7 0.7 %copy-start.5 = (f32[64]{0:T(128)S(1)}, f32[64]{0:T(128)}, u32[]{:S(2)}) copy-start(f32[64]{0:T(128)} %param.12) | copy-start | bytes 772
  0.7 0.7 %copy-start.6 = (f32[7]{0:T(128)S(1)}, f32[7]{0:T(128)}, u32[]{:S(2)}) copy-start(f32[7]{0:T(128)} %param.13) | copy-start | bytes 88
  1.3 0.8 %copy-start = (s32[640,16]{0,1:T(8,128)S(1)}, s32[640,16]{0,1:T(8,128)}, u32[]{:S(2)}) copy-start(s32[640,16]{0,1:T(8,128)} %param.9) | copy-start | bytes 122884
  2.1 0.8 %copy-start.1 = (f32[640,16]{0,1:T(8,128)S(1)}, f32[640,16]{0,1:T(8,128)}, u32[]{:S(2)}) copy-start(f32[640,16]{0,1:T(8,128)} %param.10) | copy-start | bytes 122884
  2.9 0.8 %copy-start.2 = (f32[128,64]{0,1:T(8,128)S(1)}, f32[128,64]{0,1:T(8,128)}, u32[]{:S(2)}) copy-start(f32[128,64]{0,1:T(8,128)} %param.7) | copy-start | bytes 98308

commit v3 on v2

--- a/solution.py
+++ b/solution.py
@@ -14,6 +14,7 @@
 ITERS = 4
 SUB = 8
 HALF = 256
+VMEM_BYTES = 60 * 1024 * 1024
 
 highest = lax.Precision.HIGHEST
 MESH = pl.DeviceIdType.MESH
@@ -113,7 +114,7 @@
     sublane = lax.broadcasted_iota(jnp.int32, (SUB, LEV), 0)
     own_source = jnp.dot(weighted, observed[...], precision=highest, preferred_element_type=f32)
     source[orbit, 0] = jnp.where(sublane == species, starts[...].astype(f32), own_source)
-    source_copies = []
+    source_copies = {}
     for o in range(n_orbit):
         for g, d in enumerate(groups):
             if o == 0 and g == 0:
@@ -124,7 +125,7 @@
                 device_id=(lax.rem(orbit + o, n_orbit), lax.rem(lon + d, n_lon), lat),
                 device_id_type=MESH)
             copy.start()
-            source_copies.append(copy)
+            source_copies[(o, g)] = copy
 
     gram = lax.dot_general(weighted, kernel_rows, NT_DIMS, precision=highest,
                            preferred_element_type=f32)
@@ -135,46 +136,52 @@
     pw_col = jnp.sum(jnp.where(diagonal, prior[...], 0.0), axis=1, keepdims=True)
     pw[...] = jnp.broadcast_to(pw_col, (SUB, LEV))
 
-    def build(slot):
-        def chunk(c, carry):
-            at = pl.ds(pl.multiple_of(c * LEV, LEV), LEV)
-            cell = tab[slot, 0:tile, at].astype(jnp.int32)
-            key = (cell // (CLAT * LEV)) * LEV + lax.rem(cell, LEV)
-            total = tab[slot, tile:2 * tile, at]
-            hi = total.astype(bf16).astype(f32)
-            lo = total - hi
-            rows = (lax.broadcasted_iota(jnp.int32, (HALF // 16, 16, LEV), 0) * 16
-                    + lax.broadcasted_iota(jnp.int32, (HALF // 16, 16, LEV), 1))
-            rows = rows.astype(f32).astype(bf16)
-            for half in range(CLON * LEV // HALF):
-                acc_hi = jnp.zeros((HALF // 16, 16, LEV), bf16)
-                acc_lo = jnp.zeros((HALF // 16, 16, LEV), bf16)
-                near = (key - half * HALF).astype(f32)
-                for m in range(tile):
-                    wide = lambda v: jnp.broadcast_to(v[m:m + 1, :], (16, LEV)).astype(bf16)[None]
-                    hit = rows == wide(near)
-                    acc_hi = jnp.where(hit, wide(hi), acc_hi)
-                    acc_lo = jnp.where(hit, wide(lo), acc_lo)
-                w_hi[slot, half * HALF:(half + 1) * HALF, at] = acc_hi.reshape(HALF, LEV)
-                w_lo[slot, half * HALF:(half + 1) * HALF, at] = acc_lo.reshape(HALF, LEV)
-            return carry
-
-        lax.fori_loop(0, span * rays // LEV, chunk, 0)
-
-    build(orbit)
-    for o in range(1, n_orbit):
-        tab_copies[o - 1].wait()
-        build(lax.rem(orbit + n_orbit - o, n_orbit))
-    for copy in source_copies:
-        copy.wait()
+    def build(slot, g):
+        first = source[slot, g, species:species + 1, :].astype(jnp.int32)
+        mine = [u for u in range(span) if group_of[u] == g]
+        cell = None
+        for u in mine:
+            own = tab[slot, 0:tile, u * rays:(u + 1) * rays]
+            length = tab[slot, tile:2 * tile, u * rays:(u + 1) * rays]
+            here = (first <= u) & (first + reach >= u)
+            if cell is None:
+                cell, total, there = own, length, here
+            else:
+                cell = jnp.where(here, own, cell)
+                total = jnp.where(here, length, total)
+                there = there | here
+        cell = cell.astype(jnp.int32)
+        band = lax.rem(lax.div(cell[0:1, :], LEV), CLAT)
+        at = pl.ds(g * rays, rays)
+        latkey[slot, :, at] = jnp.broadcast_to(jnp.where(there, band, -1), (SUB, rays))
+        key = lax.div(cell, CLAT * LEV) * LEV + lax.rem(cell, LEV)
+        hi = total.astype(bf16).astype(f32)
+        lo = total - hi
+        shape = (HALF // 16, 16, rays)
+        rows = lax.broadcasted_iota(jnp.int32, shape, 0) * 16 + lax.broadcasted_iota(jnp.int32, shape, 1)
+        rows = rows.astype(f32).astype(bf16)
+        for half in range(CLON * LEV // HALF):
+            acc_hi = jnp.zeros(shape, bf16)
+            acc_lo = jnp.zeros(shape, bf16)
+            near = (key - half * HALF).astype(f32)
+            for m in range(tile):
+                wide = lambda v: jnp.broadcast_to(v[m:m + 1, :], (16, rays)).astype(bf16)[None]
+                hit = rows == wide(near)
+                acc_hi = jnp.where(hit, wide(hi), acc_hi)
+                acc_lo = jnp.where(hit, wide(lo), acc_lo)
+            w_hi[slot, half * HALF:(half + 1) * HALF, at] = acc_hi.reshape(HALF, rays)
+            w_lo[slot, half * HALF:(half + 1) * HALF, at] = acc_lo.reshape(HALF, rays)
+
+    def await_source(o, g):
+        if (o, g) != (0, 0):
+            source_copies[(o, g)].wait()
 
     for o in range(n_orbit):
-        for u in range(span):
-            first = source[o, group_of[u], species:species + 1, :].astype(jnp.int32)
-            cell = tab[o, 0:1, u * rays:(u + 1) * rays].astype(jnp.int32)
-            band = lax.rem(cell // LEV, CLAT)
-            band = jnp.where((first <= u) & (first + reach >= u), band, -1)
-            latkey[o, :, u * rays:(u + 1) * rays] = jnp.broadcast_to(band, (SUB, rays))
+        if o > 0:
+            tab_copies[o - 1].wait()
+        for g in range(len(groups)):
+            await_source(o, g)
+            build(lax.rem(orbit + n_orbit - o, n_orbit), g)
 
     def back(images):
         total = None
@@ -184,7 +191,7 @@
         return total
 
     def back_orbit(o, per_group):
-        y = jnp.concatenate([per_group[group_of[u]] for u in range(span)], axis=1)
+        y = jnp.concatenate(per_group, axis=1)
         y_hi = y.astype(bf16).astype(f32)
         y_lo = y - y_hi
         band = latkey[o]
@@ -199,19 +206,23 @@
 
     def product(turn, send_sums=None, between=None):
         v_ref = ops.at[turn]
-        copies = []
         last = (CLON - 1) * LEV
-        for side, (src, dst, device) in enumerate((
-            (v_ref.at[:, last:last + LEV], lon_halo.at[turn, 0], (orbit, lax.rem(lon + 1, n_lon), lat)),
-            (v_ref.at[:, 0:LEV], lon_halo.at[turn, 1], (orbit, lax.rem(lon + n_lon - 1, n_lon), lat)),
-            (v_ref.at[(CLAT - 1) * SUB:CLAT * SUB, :], lat_halo.at[turn, 0], (orbit, lon, lax.rem(lat + 1, n_lat))),
-            (v_ref.at[0:SUB, :], lat_halo.at[turn, 1], (orbit, lon, lax.rem(lat + n_lat - 1, n_lat))),
-        )):
-            copy = pltpu.make_async_remote_copy(
+        halos = [
+            pltpu.make_async_remote_copy(
                 src_ref=src, dst_ref=dst, send_sem=halo_ssem.at[turn, side],
                 recv_sem=halo_rsem.at[turn, side], device_id=device, device_id_type=MESH)
+            for side, (src, dst, device) in enumerate((
+                (v_ref.at[(CLAT - 1) * SUB:CLAT * SUB, :], lat_halo.at[turn, 0],
+                 (orbit, lon, lax.rem(lat + 1, n_lat))),
+                (v_ref.at[0:SUB, :], lat_halo.at[turn, 1], (orbit, lon, lax.rem(lat + n_lat - 1, n_lat))),
+                (v_ref.at[:, last:last + LEV], lon_halo.at[turn, 0],
+                 (orbit, lax.rem(lon + 1, n_lon), lat)),
+                (v_ref.at[:, 0:LEV], lon_halo.at[turn, 1],
+                 (orbit, lax.rem(lon + n_lon - 1, n_lon), lat)),
+            ))
+        ]
+        for copy in halos[:2]:
             copy.start()
-            copies.append(copy)
         v = v_ref[...]
         rows = CLAT * SUB
         v_high = v.astype(bf16)
@@ -222,12 +233,11 @@
             second = jnp.dot(v_high, w_lo[o], preferred_element_type=f32)
             sums = first[0:rows] + (first[rows:] + second)
             band = latkey[o]
-            picked = jnp.zeros((SUB, span * rays), f32)
+            picked = jnp.zeros((SUB, len(groups) * rays), f32)
             for b in range(CLAT):
                 picked = jnp.where(band == b, sums[b * SUB:(b + 1) * SUB], picked)
             for g in range(len(groups)):
-                mine = [picked[:, u * rays:(u + 1) * rays] for u in range(span) if group_of[u] == g]
-                t_send[turn, o, g] = functools.reduce(lambda a, b: a + b, mine)
+                t_send[turn, o, g] = picked[:, g * rays:(g + 1) * rays]
             for k, distance in enumerate(peers):
                 if k == 0:
                     continue
@@ -240,7 +250,9 @@
             if o == 0 and send_sums is not None:
                 send_sums()
 
-        for copy in copies:
+        for copy in halos[2:]:
+            copy.start()
+        for copy in halos[:2]:
             copy.wait()
         lane = lax.broadcasted_iota(jnp.int32, (rows, LEV), 1)
         weight = jnp.concatenate([pw[...]] * CLAT, axis=0)
@@ -249,10 +261,11 @@
             here = column(c)
             south = jnp.where(lat == 0, 0.0, lat_halo[turn, 0, :, c * LEV:(c + 1) * LEV])
             north = jnp.where(lat == n_lat - 1, 0.0, lat_halo[turn, 1, :, c * LEV:(c + 1) * LEV])
-            around = column(c - 1) if c > 0 else lon_halo[turn, 0]
-            around = around + (column(c + 1) if c < CLON - 1 else lon_halo[turn, 1])
-            around = around + jnp.concatenate([south, here[:-SUB]], axis=0)
+            around = jnp.concatenate([south, here[:-SUB]], axis=0)
             around = around + jnp.concatenate([here[SUB:], north], axis=0)
+            for beside in (c - 1, c + 1):
+                if 0 <= beside < CLON:
+                    around = around + column(beside)
             around = around + jnp.where(lane == 0, 0.0, pltpu.roll(here, 1, 1))
             around = around + jnp.where(lane == LEV - 1, 0.0, pltpu.roll(here, LEV - 1, 1))
             prior_acc[:, c * LEV:(c + 1) * LEV] = weight * (6.0 * here - around)
@@ -275,7 +288,11 @@
                     image = image + gcol[t] * total[t:t + 1, :]
                 per_group.append(image)
             result = result + back_orbit(o, per_group)
-        return result
+        for copy in halos[2:]:
+            copy.wait()
+        west = result[:, :LEV] - weight * lon_halo[turn, 0]
+        east = result[:, last:] - weight * lon_halo[turn, 1]
+        return jnp.concatenate([west, result[:, LEV:last], east], axis=1)
 
     def inner(a, b):
         whole = a * b
@@ -391,9 +408,9 @@
             vmem((species, SUB, LEV), f32),
             vmem((SUB, LEV), f32),
             vmem((n_orbit, 2 * tile, rows), f32),
-            vmem((n_orbit, CLON * LEV, rows), bf16),
-            vmem((n_orbit, CLON * LEV, rows), bf16),
-            vmem((n_orbit, SUB, rows), jnp.int32),
+            vmem((n_orbit, CLON * LEV, groups * rays), bf16),
+            vmem((n_orbit, CLON * LEV, groups * rays), bf16),
+            vmem((n_orbit, SUB, groups * rays), jnp.int32),
             vmem((n_orbit, groups, SUB, rays), f32),
             vmem((ITERS,) + flat, f32),
             vmem((ITERS, 2, flat[0], LEV), f32),
@@ -409,7 +426,7 @@
             dma((ITERS,)), dma((ITERS,)),
         ],
         compiler_params=pltpu.CompilerParams(
-            collective_id=0, has_side_effects=True, vmem_limit_bytes=40 * 1024 * 1024),
+            collective_id=0, has_side_effects=True, vmem_limit_bytes=VMEM_BYTES),
     )(
         observed.T, ray_start.reshape(1, rays), tile_cells.T, tile_lengths.T,
         channel_kernel, noise_weight.reshape(1, channels), prior_weight.reshape(1, species),

time: 44.8 us -> 42.1 us (0.940)
  local copies, waits for them, and re-layouts: 3.8 us -> 1.79 us
  Pallas kernels: 40 us -> 39.5 us
    unnamed x14 -> x0, local copies, waits for them, and re-layouts: 2.98 us -> none
    transpose x1, local copies, waits for them, and re-layouts: 0.82 us -> 1.79 us  [placed(): return shaped.transpose(1, 2, 0, 3)]
    pallas_call x1, Pallas kernels: 40 us -> 39.5 us  [body(): pl.pallas_call(functools.partial(kernel, sizes), out_shape=(out, out), in...]
where the time goes in v3:
time: 42.1 us; the launch traced here: 42 us
  Pallas kernels  39.5 us (94%)
  local copies, waits for them, and re-layouts  1.79 us (4%)
  between operations  0.64 us (2%)
    pallas_call x1, Pallas kernels, body(): pl.pallas_call(functools.partial(kernel, sizes), out_shape=(out, out), in...  39.5 us
    transpose x1, local copies, waits for them, and re-layouts, placed(): return shaped.transpose(1, 2, 0, 3)  1.79 us

profile of v3, /device:TPU:0, one launch (start us, length us, event | category | flops | bytes accessed | tf_op | source)
XLA Modules:
  0.0 42.0 jit_solution(15576451145197725224)
XLA Ops:
  0.6 39.5 %shard_map.86 = (f32[64,512]{1,0:T(8,128)}, f32[64,512]{1,0:T(8,128)}) custom-call(f32[64,128]{1,0:T(8,128)} %bitcast.18, s32[1,128]{1,0:T(1,128)} %bitcast.19, s32[16,640]{1,0:T(8,128)} %bitcast.16, f32[16,640]{1,0:T(8,128)} %bitcast.17, f32[7,64]{1,0:T(8,128)} %channel_in.1, f32[1,64]{1,0:T(1,128)} %bitcast.20, f32[1,7]{1,0:T(1,128)} %bitcast.21), custom_call_target="tpu_custom_call" | custom-call | tf_op jit(solution)/shard_map/pallas_call | solution.py:393
  40.2 1.8 %copy_bitcast_fusion = (f32[7,4,8,128]{3,2,1,0:T(8,128)}, f32[7,4,8,128]{3,2,1,0:T(8,128)}) fusion(f32[8,7,4,128]{3,1,2,0:T(8,128)} %bitcast.15, f32[8,7,4,128]{3,1,2,0:T(8,128)} %bitcast.14), kind=kLoop, calls=%fused_computation | loop fusion | bytes 458752 | tf_op jit(solution)/shard_map/transpose | solution.py:437

commit v4 on v3

--- a/solution.py
+++ b/solution.py
@@ -23,14 +23,6 @@
 NT_DIMS = (((1,), (1,)), ((), ()))
 
 
-def each(count, step):
-    if count <= 16:
-        for k in range(count):
-            step(k)
-    else:
-        lax.fori_loop(0, count, lambda k, c: (step(k), c)[1], 0)
-
-
 def residues(reach, size):
     found = []
     for d in range(-reach, reach + 1):
@@ -43,7 +35,7 @@
 def kernel(sizes, observed_in, starts_in, cells_in, lengths_in, channel_in, noise_in, prior_in,
            x_out, r_out, observed, starts, cells, lengths, channel, noise, prior, load_sem,
            ck8, gcol, pw, tab, w_hi, w_lo, latkey, source, ops, lon_halo, lat_halo,
-           t_send, t_recv, d_recv, prior_acc, vec_x, vec_r, vec_w, vec_d, vec_s, vec_z,
+           t_send, t_recv, lon_sums, lat_sums, prior_acc, vec_x, vec_r, vec_w, vec_d, vec_s, vec_z,
            source_ssem, source_rsem, tab_ssem, tab_rsem, halo_ssem, halo_rsem,
            t_ssem, t_rsem, d_ssem, d_rsem):
     n_orbit, n_lon, n_lat = sizes
@@ -55,11 +47,9 @@
     groups = residues(reach, n_lon)
     peers = residues(2 * reach, n_lon)
     group_of = [groups.index((u - reach) % n_lon) for u in range(span)]
-    planes = n_lon * n_lat
     orbit = lax.axis_index("orbit")
     lon = lax.axis_index("lon")
     lat = lax.axis_index("lat")
-    place = lon * n_lat + lat
 
     barrier = pltpu.get_barrier_semaphore()
     loads = [
@@ -71,14 +61,15 @@
     for load in loads:
         load.start()
 
-    def plane_peer(k):
-        there = lax.rem(place + k, planes)
-        return (orbit, lax.div(there, n_lat), lax.rem(there, n_lat))
-
-    def greet(k):
-        pl.semaphore_signal(barrier, inc=1, device_id=plane_peer(k + 1), device_id_type=MESH)
-
-    each(planes - 1, greet)
+    def lon_peer(k):
+        return (orbit, lax.rem(lon + k, n_lon), lat)
+
+    def lat_peer(k):
+        return (orbit, lon, lax.rem(lat + k, n_lat))
+
+    for peer, count in ((lat_peer, n_lat), (lon_peer, n_lon)):
+        for k in range(1, count):
+            pl.semaphore_signal(barrier, inc=1, device_id=peer(k), device_id_type=MESH)
     for o in range(1, n_orbit):
         for d in groups:
             pl.semaphore_signal(
@@ -95,7 +86,8 @@
     tab[orbit, 0:tile, :] = own_cells.astype(f32)
     tab[orbit, tile:2 * tile, :] = totals
 
-    pl.semaphore_wait(barrier, planes - 1 + (n_orbit - 1) * len(groups))
+    pl.semaphore_wait(barrier, n_lat + n_lon - 2 + (n_orbit - 1) * len(groups))
+    sent = []
 
     tab_copies = []
     for o in range(1, n_orbit):
@@ -105,6 +97,7 @@
             device_id=(lax.rem(orbit + o, n_orbit), lon, lat), device_id_type=MESH)
         copy.start()
         tab_copies.append(copy)
+        sent.append(copy)
     for load in loads[2:]:
         load.wait()
     ck8[...] = jnp.zeros_like(ck8)
@@ -126,6 +119,7 @@
                 device_id_type=MESH)
             copy.start()
             source_copies[(o, g)] = copy
+            sent.append(copy)
 
     gram = lax.dot_general(weighted, kernel_rows, NT_DIMS, precision=highest,
                            preferred_element_type=f32)
@@ -174,11 +168,11 @@
 
     def await_source(o, g):
         if (o, g) != (0, 0):
-            source_copies[(o, g)].wait()
+            source_copies[(o, g)].wait_recv()
 
     for o in range(n_orbit):
         if o > 0:
-            tab_copies[o - 1].wait()
+            tab_copies[o - 1].wait_recv()
         for g in range(len(groups)):
             await_source(o, g)
             build(lax.rem(orbit + n_orbit - o, n_orbit), g)
@@ -204,7 +198,7 @@
         rows = CLAT * SUB
         return first[0:rows] + (first[rows:] + second)
 
-    def product(turn, send_sums=None, between=None):
+    def product(turn, pass_sums=None):
         v_ref = ops.at[turn]
         last = (CLON - 1) * LEV
         halos = [
@@ -221,6 +215,7 @@
                  (orbit, lax.rem(lon + n_lon - 1, n_lon), lat)),
             ))
         ]
+        sent.extend(halos)
         for copy in halos[:2]:
             copy.start()
         v = v_ref[...]
@@ -247,13 +242,13 @@
                     device_id=(orbit, lax.rem(lon + distance, n_lon), lat), device_id_type=MESH)
                 copy.start()
                 t_copies[o].append(copy)
-            if o == 0 and send_sums is not None:
-                send_sums()
-
+                sent.append(copy)
         for copy in halos[2:]:
             copy.start()
+        if pass_sums is not None:
+            pass_sums()
         for copy in halos[:2]:
-            copy.wait()
+            copy.wait_recv()
         lane = lax.broadcasted_iota(jnp.int32, (rows, LEV), 1)
         weight = jnp.concatenate([pw[...]] * CLAT, axis=0)
         column = lambda c: v_ref[:, c * LEV:(c + 1) * LEV]
@@ -270,12 +265,10 @@
             around = around + jnp.where(lane == LEV - 1, 0.0, pltpu.roll(here, LEV - 1, 1))
             prior_acc[:, c * LEV:(c + 1) * LEV] = weight * (6.0 * here - around)
 
-        if between is not None:
-            between()
         result = prior_acc[...]
         for o in range(n_orbit):
             for copy in t_copies[o]:
-                copy.wait()
+                copy.wait_recv()
             per_group = []
             for g, d in enumerate(groups):
                 total = t_send[turn, o, g]
@@ -289,7 +282,7 @@
                 per_group.append(image)
             result = result + back_orbit(o, per_group)
         for copy in halos[2:]:
-            copy.wait()
+            copy.wait_recv()
         west = result[:, :LEV] - weight * lon_halo[turn, 0]
         east = result[:, last:] - weight * lon_halo[turn, 1]
         return jnp.concatenate([west, result[:, LEV:last], east], axis=1)
@@ -309,25 +302,34 @@
         row = jnp.zeros((1, LEV), f32)
         for i, term in enumerate(terms):
             row = jnp.where(spot == i, term, row)
-        d_recv[turn, 0] = row
-
-    def send_dots(turn):
-        def send(k):
+        share(turn, row, lon_sums, lon_peer, n_lon, 0)
+
+    def share(turn, row, sums, peer, count, stage):
+        sums[turn, 0] = row
+        for k in range(1, count):
             pltpu.make_async_remote_copy(
-                src_ref=d_recv.at[turn, 0], dst_ref=d_recv.at[turn, k + 1],
-                send_sem=d_ssem.at[turn], recv_sem=d_rsem.at[turn],
-                device_id=plane_peer(k + 1), device_id_type=MESH).start()
-
-        each(planes - 1, send)
+                src_ref=sums.at[turn, 0], dst_ref=sums.at[turn, k],
+                send_sem=d_ssem.at[turn, stage], recv_sem=d_rsem.at[turn, stage],
+                device_id=peer(k), device_id_type=MESH).start()
+
+    def gather(turn, sums, peer, count, stage, index):
+        whole = pltpu.make_async_remote_copy(
+            src_ref=sums.at[turn, pl.ds(1, count - 1)], dst_ref=sums.at[turn, pl.ds(1, count - 1)],
+            send_sem=d_ssem.at[turn, stage], recv_sem=d_rsem.at[turn, stage],
+            device_id=peer(1), device_id_type=MESH)
+        whole.wait_recv()
+        sent.append(whole)
+        total = jnp.zeros((1, LEV), f32)
+        for f in range(count):
+            total = total + sums[turn, lax.rem(index + count - f, count)]
+        return total
+
+    def pass_dots(turn):
+        row = gather(turn, lon_sums, lon_peer, n_lon, 0, lon)
+        share(turn, row, lat_sums, lat_peer, n_lat, 1)
 
     def finish_dots(turn):
-        pltpu.make_async_remote_copy(
-            src_ref=d_recv.at[turn, pl.ds(1, planes - 1)], dst_ref=d_recv.at[turn, pl.ds(1, planes - 1)],
-            send_sem=d_ssem.at[turn], recv_sem=d_rsem.at[turn],
-            device_id=plane_peer(1), device_id_type=MESH).wait()
-        total = jnp.zeros((1, LEV), f32)
-        for f in range(planes):
-            total = total + d_recv[turn, lax.rem(place + planes - f, planes)]
+        total = gather(turn, lat_sums, lat_peer, n_lat, 1, lat)
         return [total[:, i:i + 1] for i in range(4)]
 
     images = [[jnp.where(sublane < species, source[o, g], 0.0) for g in range(len(groups))]
@@ -364,7 +366,8 @@
 
     for turn in range(ITERS - 1):
         form_dots(turn)
-        image = product(turn + 1, lambda: send_dots(turn), lambda: advance(turn))
+        image = product(turn + 1, lambda: pass_dots(turn))
+        advance(turn)
         twice = image if turn == 0 else image + kept["beta"] * vec_z[...]
         vec_z[...] = twice
         moved_on = ops[turn + 1] - kept["alpha"] * twice
@@ -373,10 +376,12 @@
         else:
             vec_w[...] = moved_on
     form_dots(ITERS - 1)
-    send_dots(ITERS - 1)
+    pass_dots(ITERS - 1)
     advance(ITERS - 1)
     x_out[...] = vec_x[...]
     r_out[...] = vec_r[...]
+    for copy in sent:
+        copy.wait_send()
 
 
 def body(sizes, observed, ray_start, tile_cells, tile_lengths, channel_kernel, noise_weight, prior_weight):
@@ -417,13 +422,14 @@
             vmem((ITERS, 2, SUB, flat[1]), f32),
             vmem((ITERS, n_orbit, groups, SUB, rays), f32),
             vmem((ITERS, peers - 1, n_orbit, groups, SUB, rays), f32),
-            vmem((ITERS, n_lon * n_lat, 1, LEV), f32),
+            vmem((ITERS, n_lon, 1, LEV), f32),
+            vmem((ITERS, n_lat, 1, LEV), f32),
         ] + [vmem(flat, f32)] * 7 + [
             dma((n_orbit, groups)), dma((n_orbit, groups)),
             dma((n_orbit,)), dma((n_orbit,)),
             dma((ITERS, 4)), dma((ITERS, 4)),
             dma((ITERS, peers, n_orbit)), dma((ITERS, peers, n_orbit)),
-            dma((ITERS,)), dma((ITERS,)),
+            dma((ITERS, 2)), dma((ITERS, 2)),
         ],
         compiler_params=pltpu.CompilerParams(
             collective_id=0, has_side_effects=True, vmem_limit_bytes=VMEM_BYTES),

time: 42.1 us -> 46 us (1.093)
  Pallas kernels: 39.5 us -> 43.4 us
    pallas_call x1, Pallas kernels: 39.5 us -> 43.4 us  [body(): pl.pallas_call(functools.partial(kernel, sizes), out_shape=(out, out), in...]
where the time goes in v4:
time: 46 us; the launch traced here: 45.8 us
  Pallas kernels  43.4 us (94%)
  local copies, waits for them, and re-layouts  1.79 us (4%)
  between operations  0.64 us (1%)
    pallas_call x1, Pallas kernels, body(): pl.pallas_call(functools.partial(kernel, sizes), out_shape=(out, out), in...  43.4 us
    transpose x1, local copies, waits for them, and re-layouts, placed(): return shaped.transpose(1, 2, 0, 3)  1.79 us

profile of v4, /device:TPU:0, one launch (start us, length us, event | category | flops | bytes accessed | tf_op | source)
XLA Modules:
  0.0 45.8 jit_solution(7290738135321466179)
XLA Ops:
  0.6 43.4 %shard_map.86 = (f32[64,512]{1,0:T(8,128)}, f32[64,512]{1,0:T(8,128)}) custom-call(f32[64,128]{1,0:T(8,128)} %bitcast.18, s32[1,128]{1,0:T(1,128)} %bitcast.19, s32[16,640]{1,0:T(8,128)} %bitcast.16, f32[16,640]{1,0:T(8,128)} %bitcast.17, f32[7,64]{1,0:T(8,128)} %channel_in.1, f32[1,64]{1,0:T(1,128)} %bitcast.20, f32[1,7]{1,0:T(1,128)} %bitcast.21), custom_call_target="tpu_custom_call" | custom-call | tf_op jit(solution)/shard_map/pallas_call | solution.py:398
  44.0 1.8 %copy_bitcast_fusion = (f32[7,4,8,128]{3,2,1,0:T(8,128)}, f32[7,4,8,128]{3,2,1,0:T(8,128)}) fusion(f32[8,7,4,128]{3,1,2,0:T(8,128)} %bitcast.15, f32[8,7,4,128]{3,1,2,0:T(8,128)} %bitcast.14), kind=kLoop, calls=%fused_computation | loop fusion | bytes 458752 | tf_op jit(solution)/shard_map/transpose | solution.py:443

commit v5 on v3

--- a/solution.py
+++ b/solution.py
@@ -43,7 +43,7 @@
 def kernel(sizes, observed_in, starts_in, cells_in, lengths_in, channel_in, noise_in, prior_in,
            x_out, r_out, observed, starts, cells, lengths, channel, noise, prior, load_sem,
            ck8, gcol, pw, tab, w_hi, w_lo, latkey, source, ops, lon_halo, lat_halo,
-           t_send, t_recv, d_recv, prior_acc, vec_x, vec_r, vec_w, vec_d, vec_s, vec_z,
+           t_send, t_recv, plane_sums, prior_acc, vec_x, vec_r, vec_w, vec_d, vec_s, vec_z,
            source_ssem, source_rsem, tab_ssem, tab_rsem, halo_ssem, halo_rsem,
            t_ssem, t_rsem, d_ssem, d_rsem):
     n_orbit, n_lon, n_lat = sizes
@@ -96,6 +96,7 @@
     tab[orbit, tile:2 * tile, :] = totals
 
     pl.semaphore_wait(barrier, planes - 1 + (n_orbit - 1) * len(groups))
+    sent = []
 
     tab_copies = []
     for o in range(1, n_orbit):
@@ -105,6 +106,7 @@
             device_id=(lax.rem(orbit + o, n_orbit), lon, lat), device_id_type=MESH)
         copy.start()
         tab_copies.append(copy)
+        sent.append(copy)
     for load in loads[2:]:
         load.wait()
     ck8[...] = jnp.zeros_like(ck8)
@@ -126,6 +128,7 @@
                 device_id_type=MESH)
             copy.start()
             source_copies[(o, g)] = copy
+            sent.append(copy)
 
     gram = lax.dot_general(weighted, kernel_rows, NT_DIMS, precision=highest,
                            preferred_element_type=f32)
@@ -174,11 +177,11 @@
 
     def await_source(o, g):
         if (o, g) != (0, 0):
-            source_copies[(o, g)].wait()
+            source_copies[(o, g)].wait_recv()
 
     for o in range(n_orbit):
         if o > 0:
-            tab_copies[o - 1].wait()
+            tab_copies[o - 1].wait_recv()
         for g in range(len(groups)):
             await_source(o, g)
             build(lax.rem(orbit + n_orbit - o, n_orbit), g)
@@ -204,7 +207,7 @@
         rows = CLAT * SUB
         return first[0:rows] + (first[rows:] + second)
 
-    def product(turn, send_sums=None, between=None):
+    def product(turn, pass_sums=None):
         v_ref = ops.at[turn]
         last = (CLON - 1) * LEV
         halos = [
@@ -221,6 +224,7 @@
                  (orbit, lax.rem(lon + n_lon - 1, n_lon), lat)),
             ))
         ]
+        sent.extend(halos)
         for copy in halos[:2]:
             copy.start()
         v = v_ref[...]
@@ -247,13 +251,14 @@
                     device_id=(orbit, lax.rem(lon + distance, n_lon), lat), device_id_type=MESH)
                 copy.start()
                 t_copies[o].append(copy)
-            if o == 0 and send_sums is not None:
-                send_sums()
+                sent.append(copy)
+            if o == 0 and pass_sums is not None:
+                pass_sums()
 
         for copy in halos[2:]:
             copy.start()
         for copy in halos[:2]:
-            copy.wait()
+            copy.wait_recv()
         lane = lax.broadcasted_iota(jnp.int32, (rows, LEV), 1)
         weight = jnp.concatenate([pw[...]] * CLAT, axis=0)
         column = lambda c: v_ref[:, c * LEV:(c + 1) * LEV]
@@ -270,12 +275,10 @@
             around = around + jnp.where(lane == LEV - 1, 0.0, pltpu.roll(here, LEV - 1, 1))
             prior_acc[:, c * LEV:(c + 1) * LEV] = weight * (6.0 * here - around)
 
-        if between is not None:
-            between()
         result = prior_acc[...]
         for o in range(n_orbit):
             for copy in t_copies[o]:
-                copy.wait()
+                copy.wait_recv()
             per_group = []
             for g, d in enumerate(groups):
                 total = t_send[turn, o, g]
@@ -289,7 +292,7 @@
                 per_group.append(image)
             result = result + back_orbit(o, per_group)
         for copy in halos[2:]:
-            copy.wait()
+            copy.wait_recv()
         west = result[:, :LEV] - weight * lon_halo[turn, 0]
         east = result[:, last:] - weight * lon_halo[turn, 1]
         return jnp.concatenate([west, result[:, LEV:last], east], axis=1)
@@ -309,25 +312,29 @@
         row = jnp.zeros((1, LEV), f32)
         for i, term in enumerate(terms):
             row = jnp.where(spot == i, term, row)
-        d_recv[turn, 0] = row
-
-    def send_dots(turn):
+        share(turn, row)
+
+    def share(turn, row):
+        plane_sums[turn, 0] = row
+
         def send(k):
             pltpu.make_async_remote_copy(
-                src_ref=d_recv.at[turn, 0], dst_ref=d_recv.at[turn, k + 1],
+                src_ref=plane_sums.at[turn, 0], dst_ref=plane_sums.at[turn, k + 1],
                 send_sem=d_ssem.at[turn], recv_sem=d_rsem.at[turn],
                 device_id=plane_peer(k + 1), device_id_type=MESH).start()
 
         each(planes - 1, send)
 
     def finish_dots(turn):
-        pltpu.make_async_remote_copy(
-            src_ref=d_recv.at[turn, pl.ds(1, planes - 1)], dst_ref=d_recv.at[turn, pl.ds(1, planes - 1)],
-            send_sem=d_ssem.at[turn], recv_sem=d_rsem.at[turn],
-            device_id=plane_peer(1), device_id_type=MESH).wait()
+        others = plane_sums.at[turn, pl.ds(1, planes - 1)]
+        whole = pltpu.make_async_remote_copy(
+            src_ref=others, dst_ref=others, send_sem=d_ssem.at[turn], recv_sem=d_rsem.at[turn],
+            device_id=plane_peer(1), device_id_type=MESH)
+        whole.wait_recv()
+        sent.append(whole)
         total = jnp.zeros((1, LEV), f32)
         for f in range(planes):
-            total = total + d_recv[turn, lax.rem(place + planes - f, planes)]
+            total = total + plane_sums[turn, lax.rem(place + planes - f, planes)]
         return [total[:, i:i + 1] for i in range(4)]
 
     images = [[jnp.where(sublane < species, source[o, g], 0.0) for g in range(len(groups))]
@@ -363,8 +370,8 @@
         kept["alpha"] = alpha
 
     for turn in range(ITERS - 1):
-        form_dots(turn)
-        image = product(turn + 1, lambda: send_dots(turn), lambda: advance(turn))
+        image = product(turn + 1, lambda: form_dots(turn))
+        advance(turn)
         twice = image if turn == 0 else image + kept["beta"] * vec_z[...]
         vec_z[...] = twice
         moved_on = ops[turn + 1] - kept["alpha"] * twice
@@ -373,10 +380,11 @@
         else:
             vec_w[...] = moved_on
     form_dots(ITERS - 1)
-    send_dots(ITERS - 1)
     advance(ITERS - 1)
     x_out[...] = vec_x[...]
     r_out[...] = vec_r[...]
+    for copy in sent:
+        copy.wait_send()
 
 
 def body(sizes, observed, ray_start, tile_cells, tile_lengths, channel_kernel, noise_weight, prior_weight):

time: 42.1 us -> 40.6 us (0.964)
  Pallas kernels: 39.5 us -> 38 us
    pallas_call x1, Pallas kernels: 39.5 us -> 38 us  [body(): pl.pallas_call(functools.partial(kernel, sizes), out_shape=(out, out), in...]
where the time goes in v5:
time: 40.6 us; the launch traced here: 40.4 us
  Pallas kernels  38 us (94%)
  local copies, waits for them, and re-layouts  1.79 us (4%)
  between operations  0.64 us (2%)
    pallas_call x1, Pallas kernels, body(): pl.pallas_call(functools.partial(kernel, sizes), out_shape=(out, out), in...  38 us
    transpose x1, local copies, waits for them, and re-layouts, placed(): return shaped.transpose(1, 2, 0, 3)  1.79 us

profile of v5, /device:TPU:0, one launch (start us, length us, event | category | flops | bytes accessed | tf_op | source)
XLA Modules:
  0.0 40.4 jit_solution(468638639062268249)
XLA Ops:
  0.6 38.0 %shard_map.86 = (f32[64,512]{1,0:T(8,128)}, f32[64,512]{1,0:T(8,128)}) custom-call(f32[64,128]{1,0:T(8,128)} %bitcast.18, s32[1,128]{1,0:T(1,128)} %bitcast.19, s32[16,640]{1,0:T(8,128)} %bitcast.16, f32[16,640]{1,0:T(8,128)} %bitcast.17, f32[7,64]{1,0:T(8,128)} %channel_in.1, f32[1,64]{1,0:T(1,128)} %bitcast.20, f32[1,7]{1,0:T(1,128)} %bitcast.21), custom_call_target="tpu_custom_call" | custom-call | tf_op jit(solution)/shard_map/pallas_call | solution.py:401
  38.6 1.8 %copy_bitcast_fusion = (f32[7,4,8,128]{3,2,1,0:T(8,128)}, f32[7,4,8,128]{3,2,1,0:T(8,128)}) fusion(f32[8,7,4,128]{3,1,2,0:T(8,128)} %bitcast.15, f32[8,7,4,128]{3,1,2,0:T(8,128)} %bitcast.14), kind=kLoop, calls=%fused_computation | loop fusion | bytes 458752 | tf_op jit(solution)/shard_map/transpose | solution.py:445

commit v6 on v5

--- a/solution.py
+++ b/solution.py
@@ -252,11 +252,11 @@
                 copy.start()
                 t_copies[o].append(copy)
                 sent.append(copy)
-            if o == 0 and pass_sums is not None:
-                pass_sums()
 
         for copy in halos[2:]:
             copy.start()
+        if pass_sums is not None:
+            pass_sums()
         for copy in halos[:2]:
             copy.wait_recv()
         lane = lax.broadcasted_iota(jnp.int32, (rows, LEV), 1)
@@ -312,11 +312,9 @@
         row = jnp.zeros((1, LEV), f32)
         for i, term in enumerate(terms):
             row = jnp.where(spot == i, term, row)
-        share(turn, row)
-
-    def share(turn, row):
         plane_sums[turn, 0] = row
 
+    def share(turn):
         def send(k):
             pltpu.make_async_remote_copy(
                 src_ref=plane_sums.at[turn, 0], dst_ref=plane_sums.at[turn, k + 1],
@@ -353,7 +351,6 @@
             alpha = norm / cross
             direction = vec_r[...]
             moved = w
-            vec_x[...] = alpha * direction
         else:
             beta = norm / kept["norm"]
             kept["beta"] = beta
@@ -361,16 +358,24 @@
             alpha = norm / kept["curvature"]
             direction = vec_r[...] + beta * vec_d[...]
             moved = w + beta * vec_s[...]
-            vec_x[...] = vec_x[...] + alpha * direction
         vec_r[...] = vec_r[...] - alpha * moved
         if turn < ITERS - 1:
             vec_d[...] = direction
             vec_s[...] = moved
         kept["norm"] = norm
         kept["alpha"] = alpha
+        if turn == ITERS - 1:
+            vec_x[...] = vec_x[...] + alpha * direction
+
+    def move_solution(turn):
+        if turn == 0:
+            vec_x[...] = kept["alpha"] * vec_d[...]
+        elif turn > 0:
+            vec_x[...] = vec_x[...] + kept["alpha"] * vec_d[...]
 
     for turn in range(ITERS - 1):
-        image = product(turn + 1, lambda: form_dots(turn))
+        form_dots(turn)
+        image = product(turn + 1, lambda: (share(turn), move_solution(turn - 1)))
         advance(turn)
         twice = image if turn == 0 else image + kept["beta"] * vec_z[...]
         vec_z[...] = twice
@@ -380,6 +385,8 @@
         else:
             vec_w[...] = moved_on
     form_dots(ITERS - 1)
+    share(ITERS - 1)
+    move_solution(ITERS - 2)
     advance(ITERS - 1)
     x_out[...] = vec_x[...]
     r_out[...] = vec_r[...]

time: 40.6 us -> 41.2 us (1.015)
  Pallas kernels: 38 us -> 38.6 us
    pallas_call x1, Pallas kernels: 38 us -> 38.6 us  [body(): pl.pallas_call(functools.partial(kernel, sizes), out_shape=(out, out), in...]
where the time goes in v6:
time: 41.2 us; the launch traced here: 41 us
  Pallas kernels  38.6 us (94%)
  local copies, waits for them, and re-layouts  1.79 us (4%)
  between operations  0.64 us (2%)
    pallas_call x1, Pallas kernels, body(): pl.pallas_call(functools.partial(kernel, sizes), out_shape=(out, out), in...  38.6 us
    transpose x1, local copies, waits for them, and re-layouts, placed(): return shaped.transpose(1, 2, 0, 3)  1.79 us

profile of v6, /device:TPU:0, one launch (start us, length us, event | category | flops | bytes accessed | tf_op | source)
XLA Modules:
  0.0 41.0 jit_solution(2126802500438975586)
XLA Ops:
  0.6 38.6 %shard_map.86 = (f32[64,512]{1,0:T(8,128)}, f32[64,512]{1,0:T(8,128)}) custom-call(f32[64,128]{1,0:T(8,128)} %bitcast.18, s32[1,128]{1,0:T(1,128)} %bitcast.19, s32[16,640]{1,0:T(8,128)} %bitcast.16, f32[16,640]{1,0:T(8,128)} %bitcast.17, f32[7,64]{1,0:T(8,128)} %channel_in.1, f32[1,64]{1,0:T(1,128)} %bitcast.20, f32[1,7]{1,0:T(1,128)} %bitcast.21), custom_call_target="tpu_custom_call" | custom-call | tf_op jit(solution)/shard_map/pallas_call | solution.py:408
  39.2 1.8 %copy_bitcast_fusion = (f32[7,4,8,128]{3,2,1,0:T(8,128)}, f32[7,4,8,128]{3,2,1,0:T(8,128)}) fusion(f32[8,7,4,128]{3,1,2,0:T(8,128)} %bitcast.15, f32[8,7,4,128]{3,1,2,0:T(8,128)} %bitcast.14), kind=kLoop, calls=%fused_computation | loop fusion | bytes 458752 | tf_op jit(solution)/shard_map/transpose | solution.py:452

commit v7 on v6

--- a/solution.py
+++ b/solution.py
@@ -375,7 +375,8 @@
 
     for turn in range(ITERS - 1):
         form_dots(turn)
-        image = product(turn + 1, lambda: (share(turn), move_solution(turn - 1)))
+        share(turn)
+        image = product(turn + 1, lambda: move_solution(turn - 1))
         advance(turn)
         twice = image if turn == 0 else image + kept["beta"] * vec_z[...]
         vec_z[...] = twice

time: 41.2 us -> 40.9 us (level)
  no operation moved by 1% of the time
where the time goes in v7:
time: 40.9 us; the launch traced here: 40.7 us
  Pallas kernels  38.3 us (94%)
  local copies, waits for them, and re-layouts  1.79 us (4%)
  between operations  0.64 us (2%)
    pallas_call x1, Pallas kernels, body(): pl.pallas_call(functools.partial(kernel, sizes), out_shape=(out, out), in...  38.3 us
    transpose x1, local copies, waits for them, and re-layouts, placed(): return shaped.transpose(1, 2, 0, 3)  1.79 us

profile of v7, /device:TPU:0, one launch (start us, length us, event | category | flops | bytes accessed | tf_op | source)
XLA Modules:
  0.0 40.7 jit_solution(10543071320171384282)
XLA Ops:
  0.6 38.3 %shard_map.86 = (f32[64,512]{1,0:T(8,128)}, f32[64,512]{1,0:T(8,128)}) custom-call(f32[64,128]{1,0:T(8,128)} %bitcast.18, s32[1,128]{1,0:T(1,128)} %bitcast.19, s32[16,640]{1,0:T(8,128)} %bitcast.16, f32[16,640]{1,0:T(8,128)} %bitcast.17, f32[7,64]{1,0:T(8,128)} %channel_in.1, f32[1,64]{1,0:T(1,128)} %bitcast.20, f32[1,7]{1,0:T(1,128)} %bitcast.21), custom_call_target="tpu_custom_call" | custom-call | tf_op jit(solution)/shard_map/pallas_call | solution.py:409
  38.9 1.8 %copy_bitcast_fusion = (f32[7,4,8,128]{3,2,1,0:T(8,128)}, f32[7,4,8,128]{3,2,1,0:T(8,128)}) fusion(f32[8,7,4,128]{3,1,2,0:T(8,128)} %bitcast.15, f32[8,7,4,128]{3,1,2,0:T(8,128)} %bitcast.14), kind=kLoop, calls=%fused_computation | loop fusion | bytes 458752 | tf_op jit(solution)/shard_map/transpose | solution.py:453
